TPU v7x, 512 devices: a whole 4x4x16 slice. The times are simulated.
512 devices in a mesh: row: 32 (over z_lo, x), col: 16 (over y, z_hi, core).
Axes of the slice: x: 4, y: 4, z: 16 (z_hi: 2, z_lo: 8; z = z_hi * 8 + z_lo), core: 2. Of those that a mesh axis runs over, the one named last changes fastest.
Arguments:
- tokens: bfloat16 [4096, 6144], P('row', 'col'), may hold values from -6 to 6
- w_up: bfloat16 [2048, 4096], P('row', 'col'), may hold values from -0.3125 to 0.3125
- up_feat: int32 [32, 64], P('row', 'col'), may hold values from 0 to 2, as said below
- up_hid: int32 [32, 64], P('row', 'col'), may hold values from 0 to 23
- up_count: int32 [32, 16], P('row', 'col'), may hold values from 2 to 4, as said below
- w_down: bfloat16 [2048, 4096], P('row', 'col'), may hold values from -0.15625 to 0.15625
- down_feat: int32 [32, 64], P('row', 'col'), may hold values from 0 to 2, as said below
- down_hid: int32 [32, 64], P('row', 'col'), may hold values from 0 to 23
- down_count: int32 [32, 16], P('row', 'col'), may hold values from 2 to 4, as said below
- grad_out: bfloat16 [4096, 6144], P('row', 'col'), may hold values from -1 to 1
Outputs:
- mixed: bfloat16 [4096, 6144], P('row', 'col')
- grad_in: bfloat16 [4096, 6144], P('row', 'col')
- grad_up: bfloat16 [2048, 4096], P('row', 'col')
- grad_down: bfloat16 [2048, 4096], P('row', 'col')
Inputs may be any that keep to these rules, and one draw needn't show every extreme that they name: For each tile, the pairs (up_feat, up_hid) of its 4 slots are distinct. `up_count`: slots at or beyond a tile's count are unused; some tile has 4. For each tile, the pairs (down_feat, down_hid) of its 4 slots are distinct. `down_count`: slots at or beyond a tile's count are unused; some tile has 4.
All inputs are finite; a program needn't handle non-finite values.
Results may differ from a plain program's by a relative error of at most 0.015.
Values may be sent and summed in bfloat16 or wider, within the bound.
A program may use at most 64 MiB of HBM per device.

v0:
```python
import jax
import jax.numpy as jnp
from jax import lax
from jax.sharding import PartitionSpec as P

H = 24576


GELU_SCALE = 0.7978845608028654
GELU_CUBIC = 0.044715


def gelu_parts(hidden_pre):
    argument = GELU_SCALE * (hidden_pre + GELU_CUBIC * hidden_pre * hidden_pre * hidden_pre)
    tanh_value = jnp.tanh(argument)
    values = 0.5 * hidden_pre * (1.0 + tanh_value)
    derivative = 0.5 * (1.0 + tanh_value) + 0.5 * hidden_pre * (
        1.0 - tanh_value * tanh_value
    ) * GELU_SCALE * (1.0 + 3.0 * GELU_CUBIC * hidden_pre * hidden_pre)
    return (values, derivative)


def encode(features, hiddens, counts, row_base):
    is_live = jnp.arange(features.shape[1], dtype=jnp.int32)[None, :] < counts
    return jnp.concatenate([features + row_base, jnp.where(is_live, hiddens, -1)], axis=1)


def block_major(values, block):
    tok_rows, width = values.shape
    return values.reshape(tok_rows, width // block, block).transpose(1, 0, 2)


def token_major(values):
    block_count, tok_rows, block = values.shape
    return values.transpose(1, 0, 2).reshape(tok_rows, block_count * block)


def pick_blocks(blocks, indices):
    tile_count, slot_count = indices.shape
    picked = jnp.take(blocks, indices.reshape(-1), axis=0)
    return picked.reshape(tile_count, slot_count, blocks.shape[1], blocks.shape[2])


def place_blocks(product, targets, target_count):
    tok_rows = product.shape[2]
    width = product.shape[3]
    flat = product.reshape(-1, tok_rows, width)
    placed = jnp.zeros((target_count, tok_rows, width), jnp.float32)
    return placed.at[targets.reshape(-1)].add(flat, mode="drop")


def up_product(token_pick, tile_values, hidden_code, hidden_blocks):
    tile_count, slot_count = hidden_code.shape
    block = tile_values.shape[0] // tile_count
    shaped = tile_values.reshape(tile_count, block, slot_count, block)
    product = jnp.einsum("rsti,risj->rstj", token_pick, shaped, preferred_element_type=jnp.float32)
    targets = jnp.where(hidden_code >= 0, hidden_code, hidden_blocks)
    return place_blocks(product, targets, hidden_blocks)


def tile_layout(partial_grads):
    tile_count, slot_count, block, _ = partial_grads.shape
    rounded_grads = partial_grads.astype(jnp.bfloat16)
    return rounded_grads.transpose(0, 2, 1, 3).reshape(tile_count * block, slot_count * block)


def total_rows(received, row_groups):
    shaped = received.reshape(row_groups, -1, received.shape[1])
    return jnp.sum(shaped, axis=0, dtype=jnp.float32).astype(jnp.bfloat16)


def shards(
    tokens, w_up, up_feat, up_hid, up_count, w_down, down_feat, down_hid, down_count, grad_out
):
    block = w_up.shape[0]
    slot_count = up_feat.shape[1]
    row_groups = lax.axis_size("row")
    col_groups = lax.axis_size("col")
    feature_width = tokens.shape[1] * col_groups
    feature_total = feature_width // block
    feature_blocks = feature_total // row_groups
    hidden_blocks = H // (block * col_groups)
    row_base = lax.axis_index("row") * feature_blocks
    up_codes = encode(up_feat, up_hid, up_count, row_base)
    down_codes = encode(down_feat, down_hid, down_count, row_base)
    token_blocks = lax.all_gather(block_major(tokens, block), "col", axis=0, tiled=True)
    up_strip, up_all = (
        lax.all_gather(w_up, "row", axis=0, tiled=True),
        lax.all_gather(up_codes, "row", axis=0, tiled=True),
    )
    token_pick = pick_blocks(token_blocks, up_all[:, :slot_count])
    hidden_pre = up_product(token_pick, up_strip, up_all[:, slot_count:], hidden_blocks)
    values, derivative = gelu_parts(hidden_pre)
    activation = values.astype(jnp.bfloat16)
    down_strip, down_all = (
        lax.all_gather(w_down, "row", axis=0, tiled=True),
        lax.all_gather(down_codes, "row", axis=0, tiled=True),
    )
    down_shaped = down_strip.reshape(row_groups, block, slot_count, block)
    down_hidden = down_all[:, slot_count:]
    down_live = down_hidden >= 0
    active_pick = pick_blocks(activation, jnp.maximum(down_hidden, 0))
    product = jnp.einsum(
        "rsti,risj->rstj", active_pick, down_shaped, preferred_element_type=jnp.float32
    )
    feature_targets = jnp.where(down_live, down_all[:, :slot_count], feature_total)
    placed = place_blocks(product, feature_targets, feature_total)
    mixed_blocks = lax.psum_scatter(
        placed.astype(jnp.bfloat16), "col", scatter_dimension=0, tiled=True
    )
    mixed = token_major(mixed_blocks)
    grad_blocks = lax.all_gather(block_major(grad_out, block), "col", axis=0, tiled=True)
    down_mask = down_live.astype(jnp.bfloat16)[:, :, None, None]
    output_pick = pick_blocks(grad_blocks, down_all[:, :slot_count]) * down_mask
    product = jnp.einsum(
        "rstj,risj->rsti", output_pick, down_shaped, preferred_element_type=jnp.float32
    )
    back = place_blocks(product, jnp.where(down_live, down_hidden, hidden_blocks), hidden_blocks)
    grad_pre = (back * derivative).astype(jnp.bfloat16)
    down_partial = tile_layout(
        jnp.einsum("rsti,rstj->rsij", active_pick, output_pick, preferred_element_type=jnp.float32)
    )
    grad_down = total_rows(
        lax.all_to_all(down_partial, "row", split_axis=0, concat_axis=0, tiled=True), row_groups
    )
    up_hidden = up_all[:, slot_count:]
    up_live = up_hidden >= 0
    up_mask = up_live.astype(jnp.bfloat16)[:, :, None, None]
    hidden_pick = pick_blocks(grad_pre, jnp.maximum(up_hidden, 0)) * up_mask
    up_shaped = up_strip.reshape(row_groups, block, slot_count, block)
    product = jnp.einsum(
        "rstj,risj->rsti", hidden_pick, up_shaped, preferred_element_type=jnp.float32
    )
    up_targets = jnp.where(up_live, up_all[:, :slot_count], feature_total)
    placed = place_blocks(product, up_targets, feature_total)
    input_blocks = lax.psum_scatter(
        placed.astype(jnp.bfloat16), "col", scatter_dimension=0, tiled=True
    )
    grad_in = token_major(input_blocks)
    up_partial = tile_layout(
        jnp.einsum("rsti,rstj->rsij", token_pick, hidden_pick, preferred_element_type=jnp.float32)
    )
    grad_up = total_rows(
        lax.all_to_all(up_partial, "row", split_axis=0, concat_axis=0, tiled=True), row_groups
    )
    return (mixed, grad_in, grad_up, grad_down)


def solution(mesh):
    return jax.shard_map(
        shards,
        mesh=mesh,
        in_specs=(
            P("row", "col"),
            P("row", "col"),
            P("row", "col"),
            P("row", "col"),
            P("row", "col"),
            P("row", "col"),
            P("row", "col"),
            P("row", "col"),
            P("row", "col"),
            P("row", "col"),
        ),
        out_specs=(P("row", "col"), P("row", "col"), P("row", "col"), P("row", "col")),
        check_vma=False,
    )
```

profile of v0, /device:TPU:6, one launch (start us, length us, event | category | flops | bytes accessed | tf_op | source)
XLA Modules:
  0.0 967.1 jit_solution(16245430436535681198)
XLA Ops:
  7.2 0.7 all-gather.11.cloned.1.call-update
  7.9 0.7 all-gather.9.cloned.1.call-update
  8.7 1.6 copy.39
  10.4 1.6 copy.34
  12.7 0.7 broadcast_add_fusion.1
  13.4 0.7 compare_select_fusion.9
  14.1 107.3 %all-gather = s32[32,1,8]{2,1,0:T(1,128)S(1)} all-gather(s32[1,1,8]{2,1,0:T(1,128)S(1)} %add_bitcast_fusion), channel_id=1, replica_groups=mesh['row'=32,'col'=16] {'row'}, dimensions={0}, use_global_device_ids=true | all-gather | bytes 1056 | tf_op jit(solution)/shard_map/all_gather | solution.py:97
  121.5 0.6 fusion.29
  122.1 0.7 broadcast_add_fusion
  123.4 0.7 compare_select_fusion.8
  124.3 0.1 reshape.244
  124.4 118.9 %all-gather.1 = s32[32,1,8]{2,1,0:T(1,128)S(1)} all-gather(s32[1,1,8]{2,1,0:T(1,128)S(1)} %add_bitcast_fusion.1), channel_id=1, replica_groups=mesh['row'=32,'col'=16] {'row'}, dimensions={0}, use_global_device_ids=true | all-gather | bytes 1056 | tf_op jit(solution)/shard_map/all_gather | solution.py:89
  243.4 0.1 reshape.234
  243.5 0.1 reshape.232
  243.6 0.1 reshape.249
  243.9 4.4 reshape.333
  248.3 200.7 %all-gather.9.cloned.1.call-done = bf16[2048,256]{1,0:T(8,128)(2,1)} async-done(((bf16[64,256]{1,0:T(8,128)(2,1)}), bf16[2048,256]{1,0:T(8,128)(2,1)}) %all-gather.9.cloned.1.call-update) | async-done | bytes 1048592 | tf_op jit(solution)/shard_map/all_gather | solution.py:88
  449.1 4.4 reshape.334
  453.5 92.1 %all-gather.13.cloned.1.call-done = bf16[96,128,64]{1,2,0:T(8,128)(2,1)} async-done(((bf16[6,128,64]{1,2,0:T(8,128)(2,1)}), bf16[96,128,64]{1,2,0:T(8,128)(2,1)}) %all-gather.13.cloned.1.call-update) | async-done | bytes 1572880 | tf_op jit(solution)/shard_map/all_gather | solution.py:112
  545.6 3.6 gather_fusion.2
  549.1 1.9 broadcast_select_fusion.1
  551.0 74.2 %all-gather.7.cloned.1.call-done = bf16[96,128,64]{1,2,0:T(8,128)(2,1)} async-done(((bf16[6,128,64]{1,2,0:T(8,128)(2,1)}), bf16[96,128,64]{1,2,0:T(8,128)(2,1)}) %all-gather.7.cloned.1.call-update) | async-done | bytes 1572880 | tf_op jit(solution)/shard_map/all_gather | solution.py:86
  625.2 3.6 gather_fusion
  628.7 2.0 broadcast_select_fusion.3
  630.8 0.2 copy-done.4
  631.0 2.8 fusion
  633.8 0.1 copy-done.2
  633.9 2.8 fusion.6
  636.7 13.5 %scatter_fusion.2 = f32[24,128,64]{1,2,0:T(8,128)S(1)} fusion(f32[24,128,64]{1,2,0:T(8,128)S(1)} %broadcast.113.clone, s32[128]{0:T(128)S(1)} %fusion.26, f32[128,128,64]{1,2,0:T(8,128)} %bitcast.47), kind=kCustom, calls=%fused_computation.6 | custom fusion | flops 1048576 | bytes 12583424 | tf_op jit(solution)/shard_map/scatter-add | solution.py:49
  650.3 13.5 %scatter_fusion = f32[24,128,64]{1,2,0:T(8,128)S(1)} fusion(f32[24,128,64]{1,2,0:T(8,128)S(1)} %broadcast.113.clone.1, s32[128]{0:T(128)S(1)} %fusion.24, f32[128,128,64]{1,2,0:T(8,128)} %bitcast.48), kind=kCustom, calls=%fused_computation.4 | custom fusion | flops 1048576 | bytes 12583424 | tf_op jit(solution)/shard_map/scatter-add | solution.py:49
  663.8 0.6 fusion.22
  664.4 2.1 gather_fusion.3
  666.6 2.0 broadcast_select_fusion
  668.6 0.2 copy-done.6
  668.8 1.3 convert_bitcast_fusion.1
  670.1 3.3 copy.42
  673.4 4.4 all_to_all.12
  677.7 5.6 all-to-all-start
  683.3 0.1 reshape.238
  683.4 0.1 reshape.243
  683.6 0.5 fusion.25
  684.1 4.3 fusion.2
  688.4 0.4 broadcast.109.clone.1
  688.8 13.7 %scatter_fusion.3 = f32[96,128,64]{1,2,0:T(8,128)S(1)} fusion(f32[96,128,64]{1,2,0:T(8,128)S(1)} %broadcast.109.clone.1, s32[128]{0:T(128)} %fusion.25, f32[128,128,64]{1,2,0:T(8,128)} %bitcast.46), kind=kCustom, calls=%fused_computation.7 | custom fusion | flops 1048576 | bytes 12583424 | tf_op jit(solution)/shard_map/scatter-add | solution.py:49
  702.5 1.5 convert_element_type.41
  704.0 1.0 gather_fusion.1
  705.0 0.3 broadcast_select_fusion.2
  705.3 2.1 copy-done.1
  707.3 1.3 convert_bitcast_fusion
  708.6 3.3 copy.43
  711.9 4.5 all_to_all.14
  716.4 17.9 %all-to-all-done = bf16[32,64,256]{2,1,0:T(8,128)(2,1)} async-done(((bf16[32,64,256]{2,1,0:T(8,128)(2,1)}), bf16[32,64,256]{2,1,0:T(8,128)(2,1)}, u32[]{:S(2)}, u32[]{:S(2)}) %all-to-all-start) | async-done | bytes 1048608 | tf_op jit(solution)/shard_map/all_to_all | solution.py:144
  734.3 7.7 all-to-all-start.1
  742.1 0.1 reshape.231
  742.2 4.4 fusion.4
  746.6 0.4 broadcast.109.clone
  747.0 13.6 %scatter_fusion.1 = f32[96,128,64]{1,2,0:T(8,128)S(1)} fusion(f32[96,128,64]{1,2,0:T(8,128)S(1)} %broadcast.109.clone, s32[128]{0:T(128)S(1)} %fusion.23, f32[128,128,64]{1,2,0:T(8,128)} %bitcast.49), kind=kCustom, calls=%fused_computation.5 | custom fusion | flops 1048576 | bytes 12583424 | tf_op jit(solution)/shard_map/scatter-add | solution.py:49
  760.6 1.5 convert_element_type.37
  762.2 82.2 %reduce-scatter.5.cloned.1.call-done = bf16[6,128,64]{1,2,0:T(8,128)(2,1)} async-done(((bf16[96,128,64]{1,2,0:T(8,128)(2,1)}), bf16[6,128,64]{1,2,0:T(8,128)(2,1)}) %reduce-scatter.5.cloned.1.call-update) | async-done | bytes 98320 | tf_op jit(solution)/shard_map/reduce_scatter | solution.py:136
  844.4 1.6 copy.45
  846.0 108.6 %reduce-scatter.3.cloned.1.call-done = bf16[6,128,64]{1,2,0:T(8,128)(2,1)} async-done(((bf16[96,128,64]{1,2,0:T(8,128)(2,1)}), bf16[6,128,64]{1,2,0:T(8,128)(2,1)}) %reduce-scatter.3.cloned.1.call-update) | async-done | bytes 98320 | tf_op jit(solution)/shard_map/reduce_scatter | solution.py:108
  954.6 1.6 copy.44
  956.3 2.0 reduce_sum.24
  958.3 2.0 reduce_sum.25
  (49 shorter events, 1.1 us)
Async XLA Ops:
  7.2 236.7 %all-gather.11.cloned.1.call-start = ((), (), s32[]{:S(2)}) async-start(), calls=%async_computation.6 | async-start | bytes 1081344 | tf_op jit(solution)/shard_map/all_gather | solution.py:96
  7.9 441.2 %all-gather.9.cloned.1.call-start = ((), (), s32[]{:S(2)}) async-start(), calls=%async_computation.5 | async-start | bytes 1081344 | tf_op jit(solution)/shard_map/all_gather | solution.py:88
  8.6 536.9 %all-gather.13.cloned.1.call-start = ((), (), s32[]{:S(2)}) async-start(), calls=%async_computation.8 | async-start | bytes 1671168 | tf_op jit(solution)/shard_map/all_gather | solution.py:112
  10.4 614.8 %all-gather.7.cloned.1.call-start = ((), (), s32[]{:S(2)}) async-start(), calls=%async_computation.4 | async-start | bytes 1671168 | tf_op jit(solution)/shard_map/all_gather | solution.py:86
  551.0 82.8 %copy-start = (bf16[128,128,64]{1,2,0:T(8,128)(2,1)}, bf16[128,128,64]{1,2,0:T(8,128)(2,1)S(1)}, u32[]{:S(2)}) copy-start(bf16[128,128,64]{1,2,0:T(8,128)(2,1)S(1)} %broadcast_select_fusion.1) | copy-start | bytes 6291460
  628.7 2.2 copy-start.4
  630.7 3.0 copy-start.5
  631.0 2.9 copy-start.2
  666.6 2.2 copy-start.6
  677.7 56.6 %all-to-all-start = ((bf16[32,64,256]{2,1,0:T(8,128)(2,1)}), bf16[32,64,256]{2,1,0:T(8,128)(2,1)}, u32[]{:S(2)}, u32[]{:S(2)}) async-start(bf16[32,64,256]{2,1,0:T(8,128)(2,1)} %all_to_all.12), calls=%async_computation.2 | async-start | bytes 2097152 | tf_op jit(solution)/shard_map/all_to_all | solution.py:144
  683.3 161.1 %reduce-scatter.5.cloned.1.call-start = ((), (), s32[]{:S(2)}) async-start(), calls=%async_computation.9 | async-start | bytes 1671168 | tf_op jit(solution)/shard_map/reduce_scatter | solution.py:136
  705.0 2.3 copy-start.1
  705.3 3.4 copy-start.7
  711.9 30.2 %copy-start.8 = (s32[32,4]{1,0:T(8,128)S(1)}, s32[32,4]{1,0:T(8,128)}, u32[]{:S(2)}) copy-start(s32[32,4]{1,0:T(8,128)} %get-tuple-element.31) | copy-start | bytes 1540
  711.9 30.3 %copy-start.3 = (bf16[32,64,4,64]{3,2,1,0:T(4,128)(2,1)S(1)}, bf16[32,64,4,64]{3,2,1,0:T(4,128)(2,1)}, u32[]{:S(2)}) copy-start(bf16[32,64,4,64]{3,2,1,0:T(4,128)(2,1)} %reshape.333) | copy-start | bytes 3145732
  734.3 224.0 %all-to-all-start.1 = ((bf16[32,64,256]{2,1,0:T(8,128)(2,1)}), bf16[32,64,256]{2,1,0:T(8,128)(2,1)}, u32[]{:S(2)}, u32[]{:S(2)}) async-start(bf16[32,64,256]{2,1,0:T(8,128)(2,1)} %all_to_all.14), calls=%async_computation.3 | async-start | bytes 2097152 | tf_op jit(solution)/shard_map/all_to_all | solution.py:124
  742.1 212.6 %reduce-scatter.3.cloned.1.call-start = ((), (), s32[]{:S(2)}) async-start(), calls=%async_computation.7 | async-start | bytes 1671168 | tf_op jit(solution)/shard_map/reduce_scatter | solution.py:108
Sparse Core Ops, SparseCore 0:
  10.1 216.8 all-gather.10
  229.1 219.9 all-gather.8
  452.9 92.6 all-gather.12
  549.3 75.8 all-gather.6
  704.1 140.1 reduce-scatter.4
  849.0 105.6 reduce-scatter.2
where the time goes:
time: 970 us; the launch traced here: 967 us
  waiting for transfers between devices  577 us (59%)
  blocking collectives  226 us (23%)
  other arithmetic  72.3 us (7%)
  local copies, waits for them, and re-layouts  45.3 us (5%)
  matrix products  16.8 us (2%)
  between operations  15.8 us (2%)
  starting transfers between devices  13.6 us (1%)
    all_gather x1, waiting for transfers between devices, shards(): lax.all_gather(w_up, 'row', axis=0, tiled=True)  201 us
    reduce_scatter x2, waiting for transfers between devices, shards(): lax.psum_scatter(placed.astype(jnp.bfloat16), 'col', scatter_dimension=0,...  191 us
    all_gather x1, blocking collectives, shards(): lax.all_gather(up_codes, 'row', axis=0, tiled=True)  119 us
    all_gather x1, blocking collectives, shards(): lax.all_gather(down_codes, 'row', axis=0, tiled=True)  107 us
    all_gather x1, waiting for transfers between devices, shards(): lax.all_gather(block_major(grad_out, block), 'col', axis=0, tiled=True)  92.1 us
    all_gather x1, waiting for transfers between devices, shards(): lax.all_gather(block_major(tokens, block), 'col', axis=0, tiled=True)  74.2 us
    scatter-add x4, other arithmetic, place_blocks(): return placed.at[targets.reshape(-1)].add(flat, mode='drop')  54.3 us
  transfers between devices with their start and end apart: 8, of which 6 were waited for; matrix products, arithmetic and copies ran while one was open for 8% of the time, Pallas kernels for 0%

commit v1 on v0

v1 whole, which is shorter than its diff:
```python
import jax
import jax.numpy as jnp
from jax import lax
from jax.experimental import pallas as pl
from jax.experimental.pallas import tpu as pltpu
from jax.sharding import PartitionSpec as P

BLK = 64
CAP = 4
TOK = 128
FEAT = 384
HB = 24
NX, NY, NZ = 4, 4, 8
UNITS = 16
ROWS = 32
GELU_SCALE = 0.7978845608028654
GELU_CUBIC = 0.044715
MESH = pl.DeviceIdType.MESH
BF = jnp.bfloat16
F32 = jnp.float32
VMEM_LIMIT = 48 << 20


def coords():
    row, col = lax.axis_index("row"), lax.axis_index("col")
    return row % 4, col // 4, row // 4, (col // 2) % 2, col % 2


def dev(x, y, zl, zh, c):
    return (zl * 4 + x, y * 4 + zh * 2 + c)


def unit(y, zh, c):
    return y * 4 + zh * 2 + c


def remote(src, dst, ss, rs, to):
    return pltpu.make_async_remote_copy(
        src_ref=src, dst_ref=dst, send_sem=ss, recv_sem=rs, device_id=to, device_id_type=MESH
    )


def greet(x, y, zl, zh, c):
    barrier = pltpu.get_barrier_semaphore()

    def hello(to):
        pl.semaphore_signal(barrier, inc=1, device_id=to, device_id_type=MESH)

    for i in range(1, 4):
        hello(dev((x + i) % 4, y, zl, zh, c))
        hello(dev(x, (y + i) % 4, zl, zh, c))
    hello(dev(x, y, zl, 1 - zh, c))
    hello(dev(x, y, zl, zh, 1 - c))

    hello(dev(x, y, (zl + 1) % 8, jnp.where(zl == NZ - 1, 1 - zh, zh), c))
    hello(dev(x, y, (zl + 7) % 8, jnp.where(zl == 0, 1 - zh, zh), c))
    pl.semaphore_wait(barrier, 10)


def gather_kernel(
    tok, grad, wup, wdn, uf, uh, uc, df, dh, dc,
    T, W, C,
    t_send, t_recv, wz_send, wz_recv, wx_send, wx_recv, cz_send, cz_recv, cx_send, cx_recv,
):
    x, y, zl, zh, c = coords()
    me = unit(y, zh, c)
    lane = lax.broadcasted_iota(jnp.int32, (1, 128), 1)
    code = jnp.zeros((1, 128), jnp.int32)
    for base, ref in ((0, uf), (4, uh), (8, df), (12, dh)):
        for s in range(CAP):
            code = jnp.where(lane == base + s, ref[0, s], code)
    C[x, zl] = code
    slot = lax.broadcasted_iota(jnp.int32, (BLK, CAP * BLK), 1) // BLK
    zero = jnp.zeros((BLK, CAP * BLK), F32)
    W[x, zl, 0:BLK] = jnp.where(slot < uc[0, 0], wup[...].astype(F32), zero).astype(BF)
    W[x, zl, BLK : 2 * BLK] = jnp.where(slot < dc[0, 0], wdn[...].astype(F32), zero).astype(BF)
    T[0, me] = tok[...].astype(F32).T.astype(BF)
    T[1, me] = grad[...].astype(F32).T.astype(BF)
    greet(x, y, zl, zh, c)

    def chain(way, j):
        to = dev(x, y, zl + (1 if way == 0 else -1), zh, c)
        return (
            remote(C.at[x, j], C.at[x, j], cz_send.at[way, j], cz_recv.at[j], to),
            remote(W.at[x, j], W.at[x, j], wz_send.at[way, j], wz_recv.at[j], to),
        )

    def chain_start(way, j):
        @pl.when((zl < NZ - 1) if way == 0 else (zl > 0))
        def _():
            for cp in chain(way, j):
                cp.start()

    def spread(j, i):
        to = dev((x + i) % 4, y, zl, zh, c)
        return remote(W.at[x, j], W.at[x, j], wx_send.at[j, i], wx_recv.at[x, j], to)

    def spread_start(j):
        for i in (1, 3, 2):
            spread(j, i).start()

    def sends(a, u):
        first = unit(y, zh, c)
        base = jnp.where(u == first, 0, 4)
        out = []
        for n, i in enumerate((1, 3, 2)):
            to = dev(x, (y + i) % 4, zl, zh, c)
            out.append(remote(T.at[a, u], T.at[a, u], t_send.at[a, base + n], t_recv.at[a, u], to))
        return out

    def core_send(a, u, n):
        return remote(
            T.at[a, u], T.at[a, u], t_send.at[a, 8 + n], t_recv.at[a, u], dev(x, y, zl, zh, 1 - c)
        )

    def z_send(a):
        return remote(
            T.at[a, me], T.at[a, me], t_send.at[a, 3], t_recv.at[a, me], dev(x, y, zl, 1 - zh, c)
        )

    def t_wait(a, u):
        remote(T.at[a, u], T.at[a, u], t_send.at[a, 7], t_recv.at[a, u], dev(x, y, zl, zh, 1 - c)).wait_recv()

    chain_start(0, zl)
    chain_start(1, zl)
    z_send(0).start()
    spread_start(zl)
    for cp in sends(0, me):
        cp.start()
    core_send(0, me, 0).start()
    z_send(1).start()
    for cp in sends(1, me):
        cp.start()
    core_send(1, me, 0).start()
    other = unit(y, 1 - zh, c)

    def near(a):
        for n, i in enumerate((1, 3, 2)):
            u = unit((y + i) % 4, zh, c)
            t_wait(a, u)
            core_send(a, u, 2 + n).start()

    def partner(a):
        t_wait(a, other)
        for cp in sends(a, other):
            cp.start()
        core_send(a, other, 1).start()

    def far(a):
        for n, i in enumerate((1, 3, 2)):
            u = unit((y + i) % 4, 1 - zh, c)
            t_wait(a, u)
            core_send(a, u, 5 + n).start()

    def step(t):
        @pl.when(zl - t >= 0)
        def _():
            j = zl - t
            for cp in chain(0, j):
                cp.wait_recv()
            chain_start(0, j)
            spread_start(j)

        @pl.when(zl + t <= NZ - 1)
        def _():
            j = zl + t
            for cp in chain(1, j):
                cp.wait_recv()
            chain_start(1, j)
            spread_start(j)

    step(1)
    step(2)
    near(0)
    step(3)
    step(4)
    partner(0)
    near(1)
    step(5)
    step(6)
    far(0)
    step(7)

    def code_send(i):
        to = dev((x + i) % 4, y, zl, zh, c)
        return remote(C.at[x], C.at[x], cx_send.at[i], cx_recv.at[x], to)

    for i in range(1, 4):
        code_send(i).start()
    partner(1)
    far(1)
    for i in range(1, 4):
        xs = (x + i) % 4
        to = dev(xs, y, zl, zh, c)
        remote(C.at[xs], C.at[xs], cx_send.at[i], cx_recv.at[xs], to).wait_recv()

        @pl.loop(0, NZ)
        def _(j):
            remote(W.at[xs, j], W.at[xs, j], wx_send.at[j, i], wx_recv.at[xs, j], to).wait_recv()

    for a in range(2):
        for u in range(8):
            t_wait(a, 2 * u + 1 - c)
    for i in range(1, 4):
        code_send(i).wait_send()

        @pl.loop(0, NZ)
        def _(j):
            spread(j, i).wait_send()

    @pl.loop(0, NZ)
    def _(j):
        @pl.when((j <= zl) & (zl < NZ - 1))
        def _():
            for cp in chain(0, j):
                cp.wait_send()

        @pl.when((j >= zl) & (zl > 0))
        def _():
            for cp in chain(1, j):
                cp.wait_send()

    for a in range(2):
        z_send(a).wait_send()
        for u in (me, other):
            for cp in sends(a, u):
                cp.wait_send()
        for n in range(8):
            core_send(a, me, n).wait_send()


def gelu_parts(v):
    t = jnp.tanh(GELU_SCALE * (v + GELU_CUBIC * v * v * v))
    values = 0.5 * v * (1.0 + t)
    slope = 0.5 * (1.0 + t) + 0.5 * v * (1.0 - t * t) * GELU_SCALE * (1.0 + 3.0 * GELU_CUBIC * v * v)
    return values, slope


def dot(a, b):
    return jnp.dot(a, b, preferred_element_type=F32)


def dot_nt(a, b):
    return lax.dot_general(a, b, (((1,), (1,)), ((), ())), preferred_element_type=F32)


def compute_kernel(T, W, C, M, G, hid, back, act, slope, gp, acc):
    hid[...] = jnp.zeros_like(hid)
    back[...] = jnp.zeros_like(back)

    def code(r, base, s):
        return C[r % 4, r // 4, 0, base + s]

    @pl.loop(0, ROWS, unroll=2)
    def _(r):
        wt = W[r % 4, r // 4, 0:BLK].astype(F32).T.astype(BF)
        for s in range(CAP):
            o = dot(wt[s * BLK : (s + 1) * BLK], T[0, r * 3 + code(r, 0, s)])
            h = code(r, 4, s)
            hid[h] = hid[h] + o

    @pl.loop(0, HB)
    def _(k):
        v, d = gelu_parts(hid[k])
        act[k] = v.astype(BF)
        slope[k] = d

    @pl.loop(0, ROWS, unroll=2)
    def _(r):
        w = W[r % 4, r // 4, BLK : 2 * BLK]
        wt = w.astype(F32).T.astype(BF)
        acc[...] = jnp.zeros_like(acc)
        grads = []
        for s in range(CAP):
            f, h = code(r, 8, s), code(r, 12, s)
            active, out = act[h], T[1, r * 3 + f]
            acc[f] = acc[f] + dot(wt[s * BLK : (s + 1) * BLK], active)
            back[h] = back[h] + dot(w[:, s * BLK : (s + 1) * BLK], out)
            grads.append(dot_nt(active, out))
        G[r % 4, r // 4, BLK : 2 * BLK] = jnp.concatenate(grads, axis=1).astype(BF)
        for f in range(3):
            M[0, r * 3 + f] = acc[f].astype(BF)

    @pl.loop(0, HB)
    def _(k):
        gp[k] = (back[k] * slope[k]).astype(BF)

    @pl.loop(0, ROWS, unroll=2)
    def _(r):
        w = W[r % 4, r // 4, 0:BLK]
        acc[...] = jnp.zeros_like(acc)
        grads = []
        for s in range(CAP):
            f, h = code(r, 0, s), code(r, 4, s)
            g = gp[h]
            acc[f] = acc[f] + dot(w[:, s * BLK : (s + 1) * BLK], g)
            grads.append(dot_nt(T[0, r * 3 + f], g))
        G[r % 4, r // 4, 0:BLK] = jnp.concatenate(grads, axis=1).astype(BF)
        for f in range(3):
            M[1, r * 3 + f] = acc[f].astype(BF)


def scatter_kernel(
    M, G, uc, dc,
    mixed, gin, gup, gdn,
    rc, s1, ry, s2, rz, rx, sz, rl, rr,
    c_send, c_recv, y_send, y_recv, z_send, z_recv, x_send, x_recv, l_send, l_recv, r_send, r_recv,
):
    x, y, zl, zh, c = coords()
    greet(x, y, zl, zh, c)

    def xs(j, i):
        xt = (x + i) % 4
        return remote(G.at[xt, j], rx.at[i - 1, j], x_send.at[j, i], x_recv.at[j, i], dev(xt, y, zl, zh, c))

    def cs(a, u):
        return remote(
            M.at[a, 2 * u + 1 - c], rc.at[a, u], c_send.at[a, u], c_recv.at[a, u], dev(x, y, zl, zh, 1 - c)
        )

    def ys(a, i, h):
        yt = (y + i) % 4
        return remote(
            s1.at[a, yt * 2 + h], ry.at[a, i - 1, h], y_send.at[a, i - 1, h], y_recv.at[a, i - 1, h],
            dev(x, yt, zl, zh, c),
        )

    def zs(a):
        return remote(s2.at[a], rz.at[a], z_send.at[a], z_recv.at[a], dev(x, y, zl, 1 - zh, c))

    for j in (0, 7):
        for i in (1, 3, 2):
            xs(j, i).start()
    for a in range(2):
        for u in range(8):
            cs(a, u).start()
    for j in (1, 6, 2, 5, 3, 4):
        for i in (1, 3, 2):
            xs(j, i).start()

    def add_core(a, u):
        cs(a, u).wait_recv()
        s1[a, u] = (M[a, 2 * u + c].astype(F32) + rc[a, u].astype(F32)).astype(BF)

    def core_stage(a):
        for h in (0, 1):
            hh = jnp.where(h == 0, 1 - zh, zh)
            for i in (1, 3, 2):
                add_core(a, ((y + i) % 4) * 2 + hh)
                ys(a, i, hh).start()
        for h in range(2):
            add_core(a, y * 2 + h)

    def y_sum(a, h):
        for i in range(1, 4):
            ys(a, i, h).wait_recv()
        total = s1[a, y * 2 + h].astype(F32)
        for i in range(3):
            total = total + ry[a, i, h].astype(F32)
        return total

    def y_stage(a):
        s2[a] = y_sum(a, 1 - zh).astype(BF)
        zs(a).start()

    def z_stage(a, out):
        own = y_sum(a, zh)
        zs(a).wait_recv()
        out[...] = (own + rz[a].astype(F32)).T.astype(BF)

    def x_sum(j):
        for i in range(1, 4):
            xs(j, i).wait_recv()
        total = G[x, j].astype(F32)
        for i in range(3):
            total = total + rx[i, j].astype(F32)
        return total

    def left(j):
        return remote(sz.at[j], rl.at[j], l_send.at[j], l_recv.at[j], dev(x, y, zl - 1, zh, c))

    def right(j):
        return remote(sz.at[j], rr.at[j], r_send.at[j], r_recv.at[j], dev(x, y, zl + 1, zh, c))

    def step(t):
        @pl.when(t < zl)
        def _():
            total = x_sum(t)

            @pl.when(zl < NZ - 1)
            def _():
                left(t).wait_recv()
                sz[t] = (total + rl[t].astype(F32)).astype(BF)

            @pl.when(zl == NZ - 1)
            def _():
                sz[t] = total.astype(BF)

            left(t).start()

        j = NZ - 1 - t

        @pl.when(j > zl)
        def _():
            total = x_sum(j)

            @pl.when(zl > 0)
            def _():
                right(j).wait_recv()
                sz[j] = (total + rr[j].astype(F32)).astype(BF)

            @pl.when(zl == 0)
            def _():
                sz[j] = total.astype(BF)

            right(j).start()

    core_stage(0)
    core_stage(1)
    step(0)
    y_stage(0)
    step(1)
    step(2)
    y_stage(1)
    for t in range(3, 7):
        step(t)
    own = x_sum(zl)

    @pl.when(zl < NZ - 1)
    def _():
        left(zl).wait_recv()

    @pl.when(zl > 0)
    def _():
        right(zl).wait_recv()

    from_left = jnp.where(zl > 0, rr[zl].astype(F32), 0.0)
    from_right = jnp.where(zl < NZ - 1, rl[zl].astype(F32), 0.0)
    own = own + from_left + from_right
    slot = lax.broadcasted_iota(jnp.int32, (BLK, CAP * BLK), 1) // BLK
    gup[...] = jnp.where(slot < uc[0, 0], own[0:BLK], 0.0).astype(BF)
    gdn[...] = jnp.where(slot < dc[0, 0], own[BLK : 2 * BLK], 0.0).astype(BF)
    z_stage(0, mixed)
    z_stage(1, gin)

    for a in range(2):
        zs(a).wait_send()
        for u in range(8):
            cs(a, u).wait_send()
        for i in range(1, 4):
            for h in range(2):
                ys(a, i, h).wait_send()

    @pl.loop(0, NZ)
    def _(j):
        for i in range(1, 4):
            xs(j, i).wait_send()

        @pl.when(j < zl)
        def _():
            left(j).wait_send()

        @pl.when(j > zl)
        def _():
            right(j).wait_send()


def vmem():
    return pl.BlockSpec(memory_space=pltpu.VMEM)


def smem():
    return pl.BlockSpec(memory_space=pltpu.SMEM)


def shards(tokens, w_up, up_feat, up_hid, up_count, w_down, down_feat, down_hid, down_count, grad_out):
    dma = pltpu.SemaphoreType.DMA
    T, W, C = pl.pallas_call(
        gather_kernel,
        name="gather",
        out_shape=(
            jax.ShapeDtypeStruct((2, UNITS, FEAT, TOK), BF),
            jax.ShapeDtypeStruct((NX, NZ, 2 * BLK, CAP * BLK), BF),
            jax.ShapeDtypeStruct((NX, NZ, 1, 128), jnp.int32),
        ),
        in_specs=[vmem()] * 4 + [smem()] * 6,
        out_specs=(vmem(),) * 3,
        scratch_shapes=[
            dma((2, 16)), dma((2, 16)), dma((2, 8)), dma((8,)), dma((8, 4)), dma((4, 8)),
            dma((2, 8)), dma((8,)), dma((4,)), dma((4,)),
        ],
        compiler_params=pltpu.CompilerParams(
            collective_id=0, has_side_effects=True, vmem_limit_bytes=VMEM_LIMIT
        ),
    )(tokens, grad_out, w_up, w_down, up_feat, up_hid, up_count, down_feat, down_hid, down_count)
    M, G = pl.pallas_call(
        compute_kernel,
        name="compute",
        out_shape=(
            jax.ShapeDtypeStruct((2, UNITS * FEAT // BLK, BLK, TOK), BF),
            jax.ShapeDtypeStruct((NX, NZ, 2 * BLK, CAP * BLK), BF),
        ),
        in_specs=[vmem(), vmem(), smem()],
        out_specs=(vmem(), vmem()),
        scratch_shapes=[
            pltpu.VMEM((HB, BLK, TOK), F32),
            pltpu.VMEM((HB, BLK, TOK), F32),
            pltpu.VMEM((HB, BLK, TOK), BF),
            pltpu.VMEM((HB, BLK, TOK), F32),
            pltpu.VMEM((HB, BLK, TOK), BF),
            pltpu.VMEM((3, BLK, TOK), F32),
        ],
        compiler_params=pltpu.CompilerParams(vmem_limit_bytes=VMEM_LIMIT),
    )(T.reshape(2, UNITS * FEAT // BLK, BLK, TOK), W, C)
    tile = (2 * BLK, CAP * BLK)
    return pl.pallas_call(
        scatter_kernel,
        name="scatter",
        out_shape=(
            jax.ShapeDtypeStruct((TOK, FEAT), BF),
            jax.ShapeDtypeStruct((TOK, FEAT), BF),
            jax.ShapeDtypeStruct((BLK, CAP * BLK), BF),
            jax.ShapeDtypeStruct((BLK, CAP * BLK), BF),
        ),
        in_specs=[vmem(), vmem(), smem(), smem()],
        out_specs=(vmem(),) * 4,
        scratch_shapes=[
            pltpu.VMEM((2, 8, FEAT, TOK), BF),
            pltpu.VMEM((2, 8, FEAT, TOK), BF),
            pltpu.VMEM((2, 3, 2, FEAT, TOK), BF),
            pltpu.VMEM((2, FEAT, TOK), BF),
            pltpu.VMEM((2, FEAT, TOK), BF),
            pltpu.VMEM((3, NZ) + tile, BF),
            pltpu.VMEM((NZ,) + tile, BF),
            pltpu.VMEM((NZ,) + tile, BF),
            pltpu.VMEM((NZ,) + tile, BF),
            dma((2, 8)), dma((2, 8)), dma((2, 3, 2)), dma((2, 3, 2)), dma((2,)), dma((2,)),
            dma((8, 4)), dma((8, 4)), dma((8,)), dma((8,)), dma((8,)), dma((8,)),
        ],
        compiler_params=pltpu.CompilerParams(
            collective_id=1, has_side_effects=True, vmem_limit_bytes=VMEM_LIMIT
        ),
    )(M.reshape(2, UNITS, FEAT, TOK), G, up_count, down_count)


def solution(mesh):
    return jax.shard_map(
        shards,
        mesh=mesh,
        in_specs=(P("row", "col"),) * 10,
        out_specs=(P("row", "col"),) * 4,
        check_vma=False,
    )
```

time: 970 us -> 199 us (0.21)
  the two profiles are of different devices: /device:TPU:6 before, /device:TPU:138 now
where the time goes in v1:
time: 199 us; the launch traced here: 198 us
  Pallas kernels  184 us (92%)
  local copies, waits for them, and re-layouts  11.9 us (6%)
    pallas_call x1, Pallas kernels, shards(): pl.pallas_call(scatter_kernel, name='scatter', out_shape=(jax.ShapeDtypeS...  111 us
    pallas_call x1, Pallas kernels, shards(): pl.pallas_call(gather_kernel, name='gather', out_shape=(jax.ShapeDtypeStr...  53.3 us
    pallas_call x1, Pallas kernels, shards(): pl.pallas_call(compute_kernel, name='compute', out_shape=(jax.ShapeDtypeS...  20.2 us
    unnamed x24, local copies, waits for them, and re-layouts  11.9 us

profile of v1, /device:TPU:138, one launch (start us, length us, event | category | flops | bytes accessed | tf_op | source)
XLA Modules:
  0.0 198.4 jit_solution(2437431369556802374)
XLA Ops:
  1.9 0.0 copy-start.2
  1.9 0.9 copy-done.2
  2.8 0.0 copy-start.3
  2.8 0.9 copy-done.3
  3.7 0.0 copy-start.4
  3.7 0.8 copy-done.4
  4.5 0.0 copy-start.5
  4.5 0.8 copy-done.5
  5.2 0.0 copy-start.6
  5.2 0.7 copy-done.6
  5.9 0.0 copy-start.7
  5.9 0.7 copy-done.7
  6.5 0.0 copy-start.8
  6.5 0.7 copy-done.8
  7.2 0.0 copy-start.9
  7.2 0.7 copy-done.9
  7.9 53.3 %gather.1 = (bf16[2,16,384,128]{3,2,1,0:T(8,128)(2,1)S(1)}, bf16[4,8,128,256]{3,2,1,0:T(8,128)(2,1)S(1)}, s32[4,8,1,128]{3,2,1,0:T(1,128)S(1)}) custom-call(bf16[128,384]{1,0:T(8,128)(2,1)S(1)} %copy-done.2, bf16[128,384]{1,0:T(8,128)(2,1)S(1)} %copy-done.3, bf16[64,256]{1,0:T(8,128)(2,1)S(1)} %copy-done.4, bf16[64,256]{1,0:T(8,128)(2,1)S(1)} %copy-done.5, ...), custom_call_target="tpu_custom_call" | custom-call | tf_op jit(solution)/shard_map/gather/pallas_call | solution.py:478
  61.2 0.0 copy-start.1
  61.2 1.6 copy-done.1
  62.8 20.2 %compute.1 = (bf16[2,96,64,128]{3,2,1,0:T(8,128)(2,1)}, bf16[4,8,128,256]{3,2,1,0:T(8,128)(2,1)S(1)}) custom-call(bf16[2,96,64,128]{3,2,1,0:T(8,128)(2,1)} %bitcast.3, bf16[4,8,128,256]{3,2,1,0:T(8,128)(2,1)S(1)} %get-tuple-element.10.W, s32[4,8,1,128]{3,2,1,0:T(1,128)S(1)} %get-tuple-element.11.C), custom_call_target="tpu_custom_call" | custom-call | tf_op jit(solution)/shard_map/compute/pallas_call | solution.py:496
  82.9 0.0 copy-start
  83.0 1.9 copy-done
  84.8 111.0 %scatter.1 = (bf16[128,384]{1,0:T(8,128)(2,1)S(1)}, bf16[128,384]{1,0:T(8,128)(2,1)S(1)}, bf16[64,256]{1,0:T(8,128)(2,1)S(1)}, bf16[64,256]{1,0:T(8,128)(2,1)S(1)}) custom-call(bf16[2,16,384,128]{3,2,1,0:T(8,128)(2,1)S(1)} %bitcast.2, bf16[4,8,128,256]{3,2,1,0:T(8,128)(2,1)S(1)} %get-tuple-element.13.G, s32[1,1]{1,0:T(1,128)S(6)} %copy.18.uc, ...), custom_call_target="tpu_custom_call" | custom-call | tf_op jit(solution)/shard_map/scatter/pallas_call | solution.py:516
  195.8 0.6 copy.20
  196.5 0.6 copy.21
  197.1 0.6 copy.22
  197.7 0.6 copy.23
Async XLA Ops:
  1.9 0.9 copy-start.2
  2.8 0.9 copy-start.3
  3.7 0.8 copy-start.4
  4.5 0.8 copy-start.5
  5.2 0.7 copy-start.6
  5.9 0.7 copy-start.7
  6.5 0.7 copy-start.8
  7.2 0.7 copy-start.9
  61.2 1.6 copy-start.1
  82.9 1.9 copy-start

commit v2 on v1

--- a/solution.py
+++ b/solution.py
@@ -328,15 +328,29 @@
     def zs(a):
         return remote(s2.at[a], rz.at[a], z_send.at[a], z_recv.at[a], dev(x, y, zl, 1 - zh, c))
 
-    for j in (0, 7):
-        for i in (1, 3, 2):
-            xs(j, i).start()
-    for a in range(2):
-        for u in range(8):
-            cs(a, u).start()
-    for j in (1, 6, 2, 5, 3, 4):
-        for i in (1, 3, 2):
-            xs(j, i).start()
+    def x_start(t):
+        @pl.when(t >= NZ - 1 - zl)
+        def _():
+            for i in (1, 3, 2):
+                xs(t - NZ + 1 + zl, i).start()
+
+        @pl.when(t >= zl)
+        def _():
+            for i in (1, 3, 2):
+                xs(NZ - 1 - t + zl, i).start()
+
+    x_start(0)
+    x_start(1)
+    for u in range(8):
+        cs(0, u).start()
+    x_start(2)
+    x_start(3)
+    for u in range(8):
+        cs(1, u).start()
+    for t in range(4, 7):
+        x_start(t)
+    for i in (1, 3, 2):
+        xs(zl, i).start()
 
     def add_core(a, u):
         cs(a, u).wait_recv()
@@ -383,25 +397,25 @@
         return remote(sz.at[j], rr.at[j], r_send.at[j], r_recv.at[j], dev(x, y, zl + 1, zh, c))
 
     def step(t):
-        @pl.when(t < zl)
-        def _():
-            total = x_sum(t)
+        @pl.when(t >= NZ - 1 - zl)
+        def _():
+            j = t - NZ + 1 + zl
+            total = x_sum(j)
 
             @pl.when(zl < NZ - 1)
             def _():
-                left(t).wait_recv()
-                sz[t] = (total + rl[t].astype(F32)).astype(BF)
+                left(j).wait_recv()
+                sz[j] = (total + rl[j].astype(F32)).astype(BF)
 
             @pl.when(zl == NZ - 1)
             def _():
-                sz[t] = total.astype(BF)
-
-            left(t).start()
-
-        j = NZ - 1 - t
-
-        @pl.when(j > zl)
-        def _():
+                sz[j] = total.astype(BF)
+
+            left(j).start()
+
+        @pl.when(t >= zl)
+        def _():
+            j = NZ - 1 - t + zl
             total = x_sum(j)
 
             @pl.when(zl > 0)

time: 199 us -> 144 us (0.72)
  the two profiles are of different devices: /device:TPU:138 before, /device:TPU:6 now
where the time goes in v2:
time: 144 us; the launch traced here: 143 us
  Pallas kernels  129 us (90%)
  local copies, waits for them, and re-layouts  11.9 us (8%)
  between operations  1.97 us (1%)
    pallas_call x1, Pallas kernels, shards(): pl.pallas_call(gather_kernel, name='gather', out_shape=(jax.ShapeDtypeStr...  63.6 us
    pallas_call x1, Pallas kernels, shards(): pl.pallas_call(scatter_kernel, name='scatter', out_shape=(jax.ShapeDtypeS...  45 us
    pallas_call x1, Pallas kernels, shards(): pl.pallas_call(compute_kernel, name='compute', out_shape=(jax.ShapeDtypeS...  20.2 us
    unnamed x24, local copies, waits for them, and re-layouts  11.9 us

profile of v2, /device:TPU:6, one launch (start us, length us, event | category | flops | bytes accessed | tf_op | source)
XLA Modules:
  0.0 142.6 jit_solution(487095712380439306)
XLA Ops:
  1.9 0.0 copy-start.2
  1.9 0.9 copy-done.2
  2.8 0.0 copy-start.3
  2.8 0.9 copy-done.3
  3.7 0.0 copy-start.4
  3.7 0.8 copy-done.4
  4.5 0.0 copy-start.5
  4.5 0.8 copy-done.5
  5.2 0.0 copy-start.6
  5.2 0.7 copy-done.6
  5.9 0.0 copy-start.7
  5.9 0.7 copy-done.7
  6.5 0.0 copy-start.8
  6.5 0.7 copy-done.8
  7.2 0.0 copy-start.9
  7.2 0.7 copy-done.9
  7.9 63.6 %gather.1 = (bf16[2,16,384,128]{3,2,1,0:T(8,128)(2,1)S(1)}, bf16[4,8,128,256]{3,2,1,0:T(8,128)(2,1)S(1)}, s32[4,8,1,128]{3,2,1,0:T(1,128)S(1)}) custom-call(bf16[128,384]{1,0:T(8,128)(2,1)S(1)} %copy-done.2, bf16[128,384]{1,0:T(8,128)(2,1)S(1)} %copy-done.3, bf16[64,256]{1,0:T(8,128)(2,1)S(1)} %copy-done.4, bf16[64,256]{1,0:T(8,128)(2,1)S(1)} %copy-done.5, ...), custom_call_target="tpu_custom_call" | custom-call | tf_op jit(solution)/shard_map/gather/pallas_call | solution.py:492
  71.4 0.0 copy-start.1
  71.5 1.6 %copy-done.1 = bf16[2,16,384,128]{3,2,1,0:T(8,128)(2,1)} copy-done((bf16[2,16,384,128]{3,2,1,0:T(8,128)(2,1)}, bf16[2,16,384,128]{3,2,1,0:T(8,128)(2,1)S(1)}, u32[]{:S(2)}) %copy-start.1) | copy-done | bytes 3145752
  73.1 20.2 %compute.1 = (bf16[2,96,64,128]{3,2,1,0:T(8,128)(2,1)}, bf16[4,8,128,256]{3,2,1,0:T(8,128)(2,1)S(1)}) custom-call(bf16[2,96,64,128]{3,2,1,0:T(8,128)(2,1)} %bitcast.3, bf16[4,8,128,256]{3,2,1,0:T(8,128)(2,1)S(1)} %get-tuple-element.10.W, s32[4,8,1,128]{3,2,1,0:T(1,128)S(1)} %get-tuple-element.11.C), custom_call_target="tpu_custom_call" | custom-call | tf_op jit(solution)/shard_map/compute/pallas_call | solution.py:510
  93.2 0.0 copy-start
  93.2 1.9 %copy-done = bf16[2,96,64,128]{3,2,1,0:T(8,128)(2,1)S(1)} copy-done((bf16[2,96,64,128]{3,2,1,0:T(8,128)(2,1)S(1)}, bf16[2,96,64,128]{3,2,1,0:T(8,128)(2,1)}, u32[]{:S(2)}) %copy-start) | copy-done | bytes 3145752
  95.1 45.0 %scatter.1 = (bf16[128,384]{1,0:T(8,128)(2,1)S(1)}, bf16[128,384]{1,0:T(8,128)(2,1)S(1)}, bf16[64,256]{1,0:T(8,128)(2,1)S(1)}, bf16[64,256]{1,0:T(8,128)(2,1)S(1)}) custom-call(bf16[2,16,384,128]{3,2,1,0:T(8,128)(2,1)S(1)} %bitcast.2, bf16[4,8,128,256]{3,2,1,0:T(8,128)(2,1)S(1)} %get-tuple-element.13.G, s32[1,1]{1,0:T(1,128)S(6)} %copy.18.uc, ...), custom_call_target="tpu_custom_call" | custom-call | tf_op jit(solution)/shard_map/scatter/pallas_call | solution.py:530
  140.1 0.6 copy.20
  140.8 0.6 copy.21
  141.4 0.6 copy.22
  142.0 0.6 copy.23
Async XLA Ops:
  1.9 0.9 copy-start.2
  2.8 0.9 copy-start.3
  3.7 0.8 copy-start.4
  4.5 0.8 copy-start.5
  5.2 0.7 copy-start.6
  5.9 0.7 copy-start.7
  6.5 0.7 copy-start.8
  7.2 0.7 copy-start.9
  71.4 1.6 %copy-start.1 = (bf16[2,16,384,128]{3,2,1,0:T(8,128)(2,1)}, bf16[2,16,384,128]{3,2,1,0:T(8,128)(2,1)S(1)}, u32[]{:S(2)}) copy-start(bf16[2,16,384,128]{3,2,1,0:T(8,128)(2,1)S(1)} %get-tuple-element.9) | copy-start | bytes 9437188
  93.2 1.9 %copy-start = (bf16[2,96,64,128]{3,2,1,0:T(8,128)(2,1)S(1)}, bf16[2,96,64,128]{3,2,1,0:T(8,128)(2,1)}, u32[]{:S(2)}) copy-start(bf16[2,96,64,128]{3,2,1,0:T(8,128)(2,1)} %get-tuple-element.12) | copy-start | bytes 9437188

commit v3 on v0

v3 whole, which is shorter than its diff:
```python
import jax
import jax.numpy as jnp
from jax import lax
from jax.experimental import pallas as pl
from jax.experimental.pallas import tpu as pltpu
from jax.sharding import PartitionSpec as P

BLK = 64
CAP = 4
TOK = 128
FEAT = 384
HALF = 192
HB = 24
NX, NY, NZ = 4, 4, 8
UNITS = 16
ROWS = 32
GELU_SCALE = 0.7978845608028654
GELU_CUBIC = 0.044715
MESH = pl.DeviceIdType.MESH
BF = jnp.bfloat16
F32 = jnp.float32
VMEM_LIMIT = 60 << 20
dma = pltpu.SemaphoreType.DMA
WTILE = (2, BLK, CAP * BLK)
UNIT = (2, HALF, TOK)
UF, UH, DF, DH = 0, 4, 8, 12


def coords():
    row, col = lax.axis_index("row"), lax.axis_index("col")
    return row % 4, col // 4, row // 4, (col // 2) % 2, col % 2


def dev(x, y, zl, zh, c):
    return (zl * 4 + x, y * 4 + zh * 2 + c)


def unit(y, zh, c):
    return y * 4 + zh * 2 + c


def remote(src, dst, ss, rs, to):
    return pltpu.make_async_remote_copy(
        src_ref=src, dst_ref=dst, send_sem=ss, recv_sem=rs, device_id=to, device_id_type=MESH
    )


def hello(x, y, zl, zh, c):
    barrier = pltpu.get_barrier_semaphore()

    def signal(to):
        pl.semaphore_signal(barrier, inc=1, device_id=to, device_id_type=MESH)

    for i in range(1, 4):
        signal(dev((x + i) % 4, y, zl, zh, c))
        signal(dev(x, (y + i) % 4, zl, zh, c))
    signal(dev(x, y, zl, 1 - zh, c))
    signal(dev(x, y, zl, zh, 1 - c))

    signal(dev(x, y, (zl + 1) % 8, jnp.where(zl == NZ - 1, 1 - zh, zh), c))
    signal(dev(x, y, (zl + 7) % 8, jnp.where(zl == 0, 1 - zh, zh), c))


def gelu_parts(v):
    t = jnp.tanh(GELU_SCALE * (v + GELU_CUBIC * v * v * v))
    values = 0.5 * v * (1.0 + t)
    slope = 0.5 * (1.0 + t) + 0.5 * v * (1.0 - t * t) * GELU_SCALE * (1.0 + 3.0 * GELU_CUBIC * v * v)
    return values, slope


def dot(a, b):
    return jnp.dot(a, b, preferred_element_type=F32)


def dot_nt(a, b):
    return lax.dot_general(a, b, (((1,), (1,)), ((), ())), preferred_element_type=F32)


def kernel(
    tok_h, grad_h, wup_h, wdn_h, uf_h, uh_h, uc_h, df_h, dh_h, dc_h,
    mixed, gin, gup, gdn,
    T0, T1, W, C, tok, grad, wup, wdn, uf, uh, uc, df, dh, dc, in_sem,
    t_send, t_recv, wz_send, wz_recv, wx_send, wx_recv, cz_send, cz_recv, cx_send, cx_recv,
    codes, table, order_v, order, p1, p2, run, act, slope, gp,
    M, G, rc, s1, ry, s2, rz, rx, sz, rl, rr, total,
    c_send, c_recv, y_sem_send, y_sem_recv, z_sem_send, z_sem_recv, x_send, x_recv,
    l_send, l_recv, r_send, r_recv,
):
    x, y, zl, zh, c = coords()
    T = (T0, T1)
    me, other = unit(y, zh, c), unit(y, 1 - zh, c)
    hbm = (tok_h, wup_h, wdn_h, uf_h, uh_h, uc_h, df_h, dh_h, dc_h, grad_h)
    local = (tok, wup, wdn, uf, uh, uc, df, dh, dc, grad)
    loads = [pltpu.make_async_copy(p, q, in_sem.at[n]) for n, (p, q) in enumerate(zip(hbm, local))]
    for cp in loads:
        cp.start()
    hello(x, y, zl, zh, c)

    def turn(a, ref):
        T[a][pl.ds(2 * me, 2)] = ref[...].astype(F32).T.astype(BF).reshape(2, 3, BLK, TOK)

    loads[0].wait()
    turn(0, tok)
    for cp in loads[1:9]:
        cp.wait()
    lane = lax.broadcasted_iota(jnp.int32, (1, 128), 1)
    code = jnp.zeros((1, 128), jnp.int32)
    for base, ref in ((0, uf), (4, uh), (8, df), (12, dh)):
        for s in range(CAP):
            code = jnp.where(lane == base + s, ref[0, s], code)
    C[x, zl] = code
    slot = lax.broadcasted_iota(jnp.int32, (BLK, CAP * BLK), 1) // BLK
    zero = jnp.zeros((BLK, CAP * BLK), F32)
    W[x, zl, 0] = jnp.where(slot < uc[0, 0], wup[...].astype(F32), zero).astype(BF)
    W[x, zl, 1] = jnp.where(slot < dc[0, 0], wdn[...].astype(F32), zero).astype(BF)
    loads[9].wait()
    turn(1, grad)
    pl.semaphore_wait(pltpu.get_barrier_semaphore(), 10)

    def chain(way, j, p):
        to = dev(x, y, zl + (1 if way == 0 else -1), zh, c)
        ref = W.at[x, j, p]
        return remote(ref, ref, wz_send.at[way, j, p], wz_recv.at[j, p], to)

    def code_chain(way, j):
        to = dev(x, y, zl + (1 if way == 0 else -1), zh, c)
        return remote(C.at[x, j], C.at[x, j], cz_send.at[way, j], cz_recv.at[j], to)

    def chain_start(way, j, p):
        @pl.when((zl < NZ - 1) if way == 0 else (zl > 0))
        def _():
            chain(way, j, p).start()
            if p == 0:
                code_chain(way, j).start()

    def spread(j, p, i):
        to = dev((x + i) % 4, y, zl, zh, c)
        ref = W.at[x, j, p]
        return remote(ref, ref, wx_send.at[j, i, p], wx_recv.at[x, j, p], to)

    def spread_start(j, p):
        for i in (1, 3, 2):
            spread(j, p, i).start()

    def t_copy(a, u, h, kind, to):
        ref = T[a].at[2 * u + h]
        return remote(ref, ref, t_send.at[a, h, kind], t_recv.at[a, 2 * u + h], to)

    def y_send(a, u, h, base):
        return [
            t_copy(a, u, h, base + n, dev(x, (y + i) % 4, zl, zh, c)) for n, i in enumerate((1, 3, 2))
        ]

    def core_send(a, u, h, n):
        return t_copy(a, u, h, 8 + n, dev(x, y, zl, zh, 1 - c))

    def z_send(a, h):
        return t_copy(a, me, h, 3, dev(x, y, zl, 1 - zh, c))

    def t_wait(a, u, h):
        t_copy(a, u, h, 7, dev(x, y, zl, zh, 1 - c)).wait_recv()

    def own(a):
        for h in range(2):
            for cp in y_send(a, me, h, 0):
                cp.start()
            core_send(a, me, h, 0).start()

    def near(a):
        for h in range(2):
            for n, i in enumerate((1, 3, 2)):
                u = unit((y + i) % 4, zh, c)
                t_wait(a, u, h)
                core_send(a, u, h, 2 + n).start()

    def partner(a, h):
        t_wait(a, other, h)
        for cp in y_send(a, other, h, 4):
            cp.start()
        core_send(a, other, h, 1).start()

    def far(a, h):
        for n, i in enumerate((1, 3, 2)):
            u = unit((y + i) % 4, 1 - zh, c)
            t_wait(a, u, h)
            core_send(a, u, h, 5 + n).start()

    def pull(t):
        for p in range(2):
            @pl.when(zl - t >= 0)
            def _():
                j = zl - t
                chain(0, j, p).wait_recv()
                if p == 0:
                    code_chain(0, j).wait_recv()
                chain_start(0, j, p)
                spread_start(j, p)

            @pl.when(zl + t <= NZ - 1)
            def _():
                j = zl + t
                chain(1, j, p).wait_recv()
                if p == 0:
                    code_chain(1, j).wait_recv()
                chain_start(1, j, p)
                spread_start(j, p)


    def xs(j, p, i):
        xt = (x + i) % 4
        return remote(
            G.at[xt, j, p], rx.at[i - 1, j, p], x_send.at[j, i, p], x_recv.at[j, i, p], dev(xt, y, zl, zh, c)
        )

    def cs(a, u):
        return remote(
            M.at[a, 2 * u + 1 - c], rc.at[a, u], c_send.at[a, u], c_recv.at[a, u], dev(x, y, zl, zh, 1 - c)
        )

    def ys(a, i, h):
        yt = (y + i) % 4
        return remote(
            s1.at[a, yt * 2 + h], ry.at[a, i - 1, h], y_sem_send.at[a, i - 1, h], y_sem_recv.at[a, i - 1, h],
            dev(x, yt, zl, zh, c),
        )

    def zs(a):
        return remote(s2.at[a], rz.at[a], z_sem_send.at[a], z_sem_recv.at[a], dev(x, y, zl, 1 - zh, c))

    def x_unit(j, p):
        for i in (1, 3, 2):
            xs(j, p, i).start()

    def add_core(a, u):
        cs(a, u).wait_recv()
        s1[a, u] = (M[a, 2 * u + c].astype(F32) + rc[a, u].astype(F32)).astype(BF)

    def core_stage(a):
        for h in (0, 1):
            hh = jnp.where(h == 0, 1 - zh, zh)
            for i in (1, 3, 2):
                add_core(a, ((y + i) % 4) * 2 + hh)
                ys(a, i, hh).start()
        for h in range(2):
            add_core(a, y * 2 + h)

    def y_sum(a, h):
        for i in range(1, 4):
            ys(a, i, h).wait_recv()
        acc = s1[a, y * 2 + h].astype(F32)
        for i in range(3):
            acc = acc + ry[a, i, h].astype(F32)
        return acc

    def y_stage(a):
        s2[a] = y_sum(a, 1 - zh).astype(BF)
        zs(a).start()

    def z_stage(a, out):
        own = y_sum(a, zh)
        zs(a).wait_recv()
        out[...] = (own + rz[a].astype(F32)).reshape(FEAT, TOK).T.astype(BF)

    def x_sum(j, p):
        for i in range(1, 4):
            xs(j, p, i).wait_recv()
        acc = G[x, j, p].astype(F32)
        for i in range(3):
            acc = acc + rx[i, j, p].astype(F32)
        return acc

    def left(j, p):
        to = dev(x, y, zl - 1, zh, c)
        return remote(sz.at[j, p], rl.at[j, p], l_send.at[j, p], l_recv.at[j, p], to)

    def right(j, p):
        to = dev(x, y, zl + 1, zh, c)
        return remote(sz.at[j, p], rr.at[j, p], r_send.at[j, p], r_recv.at[j, p], to)

    def pass_on(j, p, move, got, first):
        acc = x_sum(j, p)

        @pl.when(first)
        def _():
            sz[j, p] = acc.astype(BF)

        @pl.when(jnp.logical_not(first))
        def _():
            move(j, p).wait_recv()
            sz[j, p] = (acc + got[j, p].astype(F32)).astype(BF)

        move(j, p).start()

    def step(t, p):
        @pl.when(t >= NZ - 1 - zl)
        def _():
            pass_on(t - NZ + 1 + zl, p, left, rl, zl == NZ - 1)

        @pl.when(t >= zl)
        def _():
            pass_on(NZ - 1 - t + zl, p, right, rr, zl == 0)


    def code(r, k):
        return codes[r % 4, r // 4, 0, k]

    def forward(j, xx):
        r = j * 4 + xx
        wt = W[xx, j, 0].astype(F32).T.astype(BF)
        for s in range(CAP):
            p1[r * CAP + s] = dot(wt[s * BLK : (s + 1) * BLK], T[0][r, code(r, UF + s)])

    def backward(j, xx):
        r = j * 4 + xx
        w = W[xx, j, 1]
        for s in range(CAP):
            p2[r * CAP + s] = dot(w[:, s * BLK : (s + 1) * BLK], T[1][r, code(r, DF + s)])

    def slot_masks(r, base):
        lane = lax.broadcasted_iota(jnp.int32, (1, CAP * BLK), 1) // BLK
        which = jnp.zeros((1, CAP * BLK), jnp.int32)
        for s in range(CAP):
            which = jnp.where(lane == s, code(r, base + s), which)
        return [jnp.where(which == f, 1.0, 0.0).astype(BF) for f in range(3)]

    def mixed_tile(r):
        w = W[r % 4, r // 4, 1].astype(F32)
        w = jnp.concatenate([w[:, s * BLK : (s + 1) * BLK].T for s in range(CAP)], axis=1).astype(BF)
        lhs = jnp.concatenate([w * m for m in slot_masks(r, DF)], axis=0)
        rhs = jnp.concatenate([act[code(r, DH + s)] for s in range(CAP)], axis=0)
        M[0, r // 2, r % 2] = dot(lhs, rhs).astype(BF)

    def input_tile(r):
        w = W[r % 4, r // 4, 0]
        lhs = jnp.concatenate([w * m for m in slot_masks(r, UF)], axis=0)
        rhs = jnp.concatenate([gp[code(r, UH + s)] for s in range(CAP)], axis=0)
        M[1, r // 2, r % 2] = dot(lhs, rhs).astype(BF)

    def down_tile(j, xx):
        r = j * 4 + xx
        parts = [dot_nt(act[code(r, DH + s)], T[1][r, code(r, DF + s)]) for s in range(CAP)]
        G[xx, j, 1] = jnp.concatenate(parts, axis=1).astype(BF)

    def up_tile(j, xx):
        r = j * 4 + xx
        parts = [dot_nt(T[0][r, code(r, UF + s)], gp[code(r, UH + s)]) for s in range(CAP)]
        G[xx, j, 0] = jnp.concatenate(parts, axis=1).astype(BF)

    def sort_slots(base, row):
        col_at = lax.broadcasted_iota(jnp.int32, (ROWS, 1), 0)
        lane128 = lax.broadcasted_iota(jnp.int32, (ROWS, 128), 1)
        keys = table[0:ROWS, :]
        turned = table[...].T
        perm = jnp.zeros((1, 128), jnp.int32)
        sorted_keys = jnp.zeros((1, 128), jnp.int32)
        below = jnp.zeros((1, 128), jnp.int32)
        for s in range(CAP):
            mine = jnp.sum(jnp.where(lane128 == base + s, keys, 0), axis=1, keepdims=True)
            rank = jnp.zeros((ROWS, 1), jnp.int32)
            for o in range(CAP):
                theirs = turned[base + o : base + o + 1, :]
                first = (theirs < mine) | ((theirs == mine) & (o * ROWS + lane128 < s * ROWS + col_at))
                first = first & (lane128 < ROWS)
                rank = rank + jnp.sum(jnp.where(first, 1, 0), axis=1, keepdims=True)
            here = rank == lane128
            perm = perm + jnp.sum(jnp.where(here, col_at * CAP + s, 0), axis=0, keepdims=True)
            sorted_keys = sorted_keys + jnp.sum(jnp.where(here, mine, 0), axis=0, keepdims=True)
            below = below + jnp.sum(jnp.where(mine < lane128, 1, 0), axis=0, keepdims=True)
        order_v[row : row + 1] = perm
        order_v[row + 1 : row + 2] = sorted_keys
        order_v[row + 2 : row + 3] = below

    def segment_sums(src, row):
        def add(i, carry):
            keep = order[row + 1, i] == order[row + 1, jnp.maximum(i - 1, 0)]
            carry = jnp.where(keep, carry, 0.0) + src[order[row, i]]
            run[i + 1] = carry
            return carry

        lax.fori_loop(0, ROWS * CAP, add, jnp.zeros((BLK, TOK), F32), unroll=4)

    def segment(row, k):
        last = order[row + 2, k + 1]
        return jnp.where(last > order[row + 2, k], run[last], 0.0)

    def tiles(fn):
        @pl.loop(0, NZ)
        def _(j):
            for xx in range(NX):
                fn(j, xx)

    def units(fn, a, mine):
        @pl.loop(0, 8)
        def _(v):
            u = 2 * v + (c if mine else 1 - c)
            for h in range(2):
                fn(2 * u + h)
            if not mine:
                cs(a, v).start()

    def wave(fn, p):
        def one(j):
            for xx in range(NX):
                fn(j, xx)
            x_unit(j, p)

        @pl.loop(0, NZ - 1)
        def _(t):
            @pl.when(t >= NZ - 1 - zl)
            def _():
                one(t - NZ + 1 + zl)

            @pl.when(t >= zl)
            def _():
                one(NZ - 1 - t + zl)

        one(zl)
    for p in range(2):
        chain_start(0, zl, p)
        chain_start(1, zl, p)
        if p == 0:
            z_send(0, 0).start()
        spread_start(zl, p)
    own(0)
    z_send(0, 1).start()
    own(1)

    pull(1)
    pull(2)
    near(0)
    pull(3)
    z_send(1, 0).start()
    partner(0, 0)
    pull(4)
    partner(0, 1)
    near(1)
    z_send(1, 1).start()
    pull(5)
    far(0, 0)
    pull(6)
    far(0, 1)
    pull(7)

    def code_send(i):
        to = dev((x + i) % 4, y, zl, zh, c)
        return remote(C.at[x], C.at[x], cx_send.at[i], cx_recv.at[x], to)

    for i in range(1, 4):
        code_send(i).start()
    partner(1, 0)
    for i in range(1, 4):
        xs_ = (x + i) % 4
        to = dev(xs_, y, zl, zh, c)
        remote(C.at[xs_], C.at[xs_], cx_send.at[i], cx_recv.at[xs_], to).wait_recv()
    to_smem = pltpu.make_async_copy(C, codes, in_sem.at[0])
    to_smem.start()
    table[...] = jnp.zeros_like(table)
    order_v[...] = jnp.zeros_like(order_v)
    run[0] = jnp.zeros((BLK, TOK), F32)
    for r in range(ROWS):
        table[r : r + 1] = C[r % 4, r // 4]
    sort_slots(UH, 0)
    sort_slots(DH, 3)
    order_copy = pltpu.make_async_copy(order_v, order, in_sem.at[1])
    order_copy.start()
    for i in range(1, 4):
        xs_ = (x + i) % 4
        to = dev(xs_, y, zl, zh, c)

        @pl.loop(0, NZ)
        def _(j):
            for p in range(2):
                ref = W.at[xs_, j, p]
                remote(ref, ref, wx_send.at[j, i, p], wx_recv.at[xs_, j, p], to).wait_recv()

    def core_wait(a):
        @pl.loop(0, 8)
        def _(v):
            for h in range(2):
                t_wait(a, 2 * v + 1 - c, h)

    core_wait(0)
    to_smem.wait()
    order_copy.wait()
    tiles(forward)
    partner(1, 1)
    far(1, 0)
    segment_sums(p1, 0)

    @pl.loop(0, HB)
    def _(k):
        v, d = gelu_parts(segment(0, k))
        act[k] = v.astype(BF)
        slope[k] = d

    far(1, 1)
    units(mixed_tile, 0, False)
    units(mixed_tile, 0, True)
    core_wait(1)
    tiles(backward)
    core_stage(0)
    segment_sums(p2, 3)

    @pl.loop(0, HB)
    def _(k):
        gp[k] = (segment(3, k) * slope[k]).astype(BF)

    wave(up_tile, 0)
    y_stage(0)
    step(0, 0)
    wave(down_tile, 1)
    step(1, 0)
    units(input_tile, 1, False)
    step(2, 0)
    units(input_tile, 1, True)
    step(3, 0)
    step(0, 1)
    core_stage(1)
    step(4, 0)
    step(1, 1)
    step(5, 0)
    step(2, 1)
    y_stage(1)
    step(6, 0)
    for t in range(3, 7):
        step(t, 1)
    owns = []
    for p in range(2):
        total[...] = x_sum(zl, p)

        @pl.when(zl < NZ - 1)
        def _():
            left(zl, p).wait_recv()
            total[...] += rl[zl, p].astype(F32)

        @pl.when(zl > 0)
        def _():
            right(zl, p).wait_recv()
            total[...] += rr[zl, p].astype(F32)

        owns.append(total[...])
    slot = lax.broadcasted_iota(jnp.int32, (BLK, CAP * BLK), 1) // BLK
    gup[...] = jnp.where(slot < uc[0, 0], owns[0], 0.0).astype(BF)
    gdn[...] = jnp.where(slot < dc[0, 0], owns[1], 0.0).astype(BF)
    z_stage(0, mixed)
    z_stage(1, gin)

    for i in range(1, 4):
        code_send(i).wait_send()

        @pl.loop(0, NZ)
        def _(j):
            for p in range(2):
                spread(j, p, i).wait_send()

    @pl.loop(0, NZ)
    def _(j):
        @pl.when((j <= zl) & (zl < NZ - 1))
        def _():
            code_chain(0, j).wait_send()
            for p in range(2):
                chain(0, j, p).wait_send()

        @pl.when((j >= zl) & (zl > 0))
        def _():
            code_chain(1, j).wait_send()
            for p in range(2):
                chain(1, j, p).wait_send()

    for a in range(2):
        for h in range(2):
            z_send(a, h).wait_send()
            for u, base in ((me, 0), (other, 4)):
                for cp in y_send(a, u, h, base):
                    cp.wait_send()
            for n in range(8):
                core_send(a, me, h, n).wait_send()

    for a in range(2):
        zs(a).wait_send()
        for u in range(8):
            cs(a, u).wait_send()
        for i in range(1, 4):
            for h in range(2):
                ys(a, i, h).wait_send()

    @pl.loop(0, NZ)
    def _(j):
        for p in range(2):
            for i in range(1, 4):
                xs(j, p, i).wait_send()

        @pl.when(j < zl)
        def _():
            for p in range(2):
                left(j, p).wait_send()

        @pl.when(j > zl)
        def _():
            for p in range(2):
                right(j, p).wait_send()


def vmem():
    return pl.BlockSpec(memory_space=pltpu.VMEM)


def shards(tokens, w_up, up_feat, up_hid, up_count, w_down, down_feat, down_hid, down_count, grad_out):
    V, S, I32 = pltpu.VMEM, pltpu.SMEM, jnp.int32
    scratch = [
        V((ROWS, 3, BLK, TOK), BF), V((ROWS, 3, BLK, TOK), BF), V((NX, NZ) + WTILE, BF), V((NX, NZ, 1, 128), I32),
        V((TOK, FEAT), BF), V((TOK, FEAT), BF), V((BLK, CAP * BLK), BF), V((BLK, CAP * BLK), BF),
        S((1, CAP), I32), S((1, CAP), I32), S((1, 1), I32), S((1, CAP), I32), S((1, CAP), I32), S((1, 1), I32),
        dma((10,)),
        dma((2, 2, 16)), dma((2, ROWS)), dma((2, NZ, 2)), dma((NZ, 2)), dma((NZ, 4, 2)), dma((NX, NZ, 2)),
        dma((2, NZ)), dma((NZ,)), dma((4,)), dma((4,)),
        S((NX, NZ, 1, 128), I32), V((128, 128), I32), V((8, 128), I32), S((8, 128), I32),
        V((ROWS * CAP, BLK, TOK), F32), V((ROWS * CAP, BLK, TOK), F32), V((ROWS * CAP + 1, BLK, TOK), F32),
        V((HB, BLK, TOK), BF), V((HB, BLK, TOK), F32), V((HB, BLK, TOK), BF),
        V((2, UNITS) + UNIT, BF), V((NX, NZ) + WTILE, BF),
        V((2, 8) + UNIT, BF), V((2, 8) + UNIT, BF), V((2, 3, 2) + UNIT, BF), V((2,) + UNIT, BF), V((2,) + UNIT, BF),
        V((3, NZ) + WTILE, BF), V((NZ,) + WTILE, BF), V((NZ,) + WTILE, BF), V((NZ,) + WTILE, BF),
        V((BLK, CAP * BLK), F32),
        dma((2, 8)), dma((2, 8)), dma((2, 3, 2)), dma((2, 3, 2)), dma((2,)), dma((2,)),
        dma((8, 4, 2)), dma((8, 4, 2)), dma((8, 2)), dma((8, 2)), dma((8, 2)), dma((8, 2)),
    ]
    return pl.pallas_call(
        kernel,
        name="ffn",
        out_shape=(
            jax.ShapeDtypeStruct((TOK, FEAT), BF),
            jax.ShapeDtypeStruct((TOK, FEAT), BF),
            jax.ShapeDtypeStruct((BLK, CAP * BLK), BF),
            jax.ShapeDtypeStruct((BLK, CAP * BLK), BF),
        ),
        in_specs=[pl.BlockSpec(memory_space=pltpu.HBM)] * 10,
        out_specs=(vmem(),) * 4,
        scratch_shapes=scratch,
        compiler_params=pltpu.CompilerParams(
            collective_id=0, has_side_effects=True, vmem_limit_bytes=VMEM_LIMIT
        ),
    )(tokens, grad_out, w_up, w_down, up_feat, up_hid, up_count, down_feat, down_hid, down_count)


def solution(mesh):
    return jax.shard_map(
        shards,
        mesh=mesh,
        in_specs=(P("row", "col"),) * 10,
        out_specs=(P("row", "col"),) * 4,
        check_vma=False,
    )
```

time: 970 us -> 129 us (0.13)
  the two profiles are of different devices: /device:TPU:6 before, /device:TPU:8 now
where the time goes in v3:
time: 129 us
  Pallas kernels  123 us (95%)
  local copies, waits for them, and re-layouts  3.72 us (3%)
  between operations  1.95 us (2%)
    pallas_call x1, Pallas kernels, shards(): pl.pallas_call(kernel, name='ffn', out_shape=(jax.ShapeDtypeStruct((TOK,...  123 us
    unnamed x10, local copies, waits for them, and re-layouts  3.72 us

profile of v3, /device:TPU:8, one launch (start us, length us, event | category | flops | bytes accessed | tf_op | source)
XLA Modules:
  0.0 128.7 jit_solution(607707191403999374)
XLA Ops:
  1.9 123.0 %ffn.1 = (bf16[128,384]{1,0:T(8,128)(2,1)}, bf16[128,384]{1,0:T(8,128)(2,1)}, bf16[64,256]{1,0:T(8,128)(2,1)}, bf16[64,256]{1,0:T(8,128)(2,1)}) custom-call(bf16[128,384]{1,0:T(8,128)(2,1)} %tok_h.1, bf16[128,384]{1,0:T(8,128)(2,1)} %grad_h.1, bf16[64,256]{1,0:T(8,128)(2,1)} %wup_h.1, bf16[64,256]{1,0:T(8,128)(2,1)} %wdn_h.1, s32[1,4]{1,0:T(1,128)} %uf_h.1, ...), custom_call_target="tpu_custom_call" | custom-call | tf_op jit(solution)/shard_map/ffn/pallas_call | solution.py:627
  124.9 0.0 copy-start
  124.9 1.6 %copy.20 = bf16[128,384]{1,0:T(8,128)(2,1)} copy(bf16[128,384]{1,0:T(8,128)(2,1)} %get-tuple-element.8) | data formatting | bytes 196608
  126.5 0.0 copy-done
  126.5 0.0 copy-start.2
  126.5 0.6 copy.21
  127.2 0.1 copy-done.2
  127.3 0.0 copy-start.1
  127.3 0.6 copy.22
  127.9 0.2 copy-done.1
  128.0 0.6 copy.23
Async XLA Ops:
  124.9 1.6 %copy-start = (bf16[128,384]{1,0:T(8,128)(2,1)S(1)}, bf16[128,384]{1,0:T(8,128)(2,1)}, u32[]{:S(2)}) copy-start(bf16[128,384]{1,0:T(8,128)(2,1)} %get-tuple-element.9) | copy-start | bytes 294916
  126.5 0.8 copy-start.2
  127.3 0.8 copy-start.1

commit v4 on v3

--- a/solution.py
+++ b/solution.py
@@ -82,7 +82,7 @@
     T0, T1, W, C, tok, grad, wup, wdn, uf, uh, uc, df, dh, dc, in_sem,
     t_send, t_recv, wz_send, wz_recv, wx_send, wx_recv, cz_send, cz_recv, cx_send, cx_recv,
     codes, table, order_v, order, p1, p2, run, act, slope, gp,
-    M, G, rc, s1, ry, s2, rz, rx, sz, rl, rr, total,
+    lhs, M, G, rc, s1, ry, s2, rz, rx, sz, rl, rr, total,
     c_send, c_recv, y_sem_send, y_sem_recv, z_sem_send, z_sem_recv, x_send, x_recv,
     l_send, l_recv, r_send, r_recv,
 ):
@@ -323,18 +323,25 @@
             which = jnp.where(lane == s, code(r, base + s), which)
         return [jnp.where(which == f, 1.0, 0.0).astype(BF) for f in range(3)]
 
-    def mixed_tile(r):
+    def expand(r):
+        w = W[r % 4, r // 4, 0]
+        lhs[1, r] = jnp.concatenate([w * m for m in slot_masks(r, UF)], axis=0)
         w = W[r % 4, r // 4, 1].astype(F32)
         w = jnp.concatenate([w[:, s * BLK : (s + 1) * BLK].T for s in range(CAP)], axis=1).astype(BF)
-        lhs = jnp.concatenate([w * m for m in slot_masks(r, DF)], axis=0)
+        lhs[0, r] = jnp.concatenate([w * m for m in slot_masks(r, DF)], axis=0)
+
+    def mixed_tile(r):
         rhs = jnp.concatenate([act[code(r, DH + s)] for s in range(CAP)], axis=0)
-        M[0, r // 2, r % 2] = dot(lhs, rhs).astype(BF)
+        M[0, r // 2, r % 2] = dot(lhs[0, r], rhs).astype(BF)
 
     def input_tile(r):
-        w = W[r % 4, r // 4, 0]
-        lhs = jnp.concatenate([w * m for m in slot_masks(r, UF)], axis=0)
         rhs = jnp.concatenate([gp[code(r, UH + s)] for s in range(CAP)], axis=0)
-        M[1, r // 2, r % 2] = dot(lhs, rhs).astype(BF)
+        M[1, r // 2, r % 2] = dot(lhs[1, r], rhs).astype(BF)
+
+    def expand_all():
+        @pl.loop(0, ROWS, unroll=2)
+        def _(r):
+            expand(r)
 
     def down_tile(j, xx):
         r = j * 4 + xx
@@ -383,15 +390,16 @@
         last = order[row + 2, k + 1]
         return jnp.where(last > order[row + 2, k], run[last], 0.0)
 
-    def tiles(fn):
-        @pl.loop(0, NZ)
+    def tiles(fn, start=0, end=NZ):
+        @pl.loop(start, end)
         def _(j):
             for xx in range(NX):
                 fn(j, xx)
 
     def units(fn, a, mine):
         @pl.loop(0, 8)
-        def _(v):
+        def _(n):
+            v = 2 * (n % 4) + jnp.where(n < 4, 1 - zh, zh)
             u = 2 * v + (c if mine else 1 - c)
             for h in range(2):
                 fn(2 * u + h)
@@ -421,10 +429,65 @@
         if p == 0:
             z_send(0, 0).start()
         spread_start(zl, p)
+    def code_send(i):
+        to = dev((x + i) % 4, y, zl, zh, c)
+        return remote(C.at[x], C.at[x], cx_send.at[i], cx_recv.at[x], to)
+
+    def code_sends():
+        for i in range(1, 4):
+            code_send(i).start()
+
+    to_smem = pltpu.make_async_copy(C, codes, in_sem.at[0])
+    order_copy = pltpu.make_async_copy(order_v, order, in_sem.at[1])
+
+    def settle():
+        for i in range(1, 4):
+            xt = (x + i) % 4
+            to = dev(xt, y, zl, zh, c)
+            remote(C.at[xt], C.at[xt], cx_send.at[i], cx_recv.at[xt], to).wait_recv()
+        to_smem.start()
+        table[...] = jnp.zeros_like(table)
+        order_v[...] = jnp.zeros_like(order_v)
+        run[0] = jnp.zeros((BLK, TOK), F32)
+        for r in range(ROWS):
+            table[r : r + 1] = C[r % 4, r // 4]
+        sort_slots(UH, 0)
+        sort_slots(DH, 3)
+        order_copy.start()
+        for i in range(1, 4):
+            xt = (x + i) % 4
+            to = dev(xt, y, zl, zh, c)
+
+            @pl.loop(0, NZ)
+            def _(j):
+                for p in range(2):
+                    ref = W.at[xt, j, p]
+                    remote(ref, ref, wx_send.at[j, i, p], wx_recv.at[xt, j, p], to).wait_recv()
+
+        to_smem.wait()
+        order_copy.wait()
+
+    def core_wait(a):
+        @pl.loop(0, 8)
+        def _(v):
+            for h in range(2):
+                t_wait(a, 2 * v + 1 - c, h)
+
+    def gelu():
+        @pl.loop(0, HB)
+        def _(k):
+            v, d = gelu_parts(segment(0, k))
+            act[k] = v.astype(BF)
+            slope[k] = d
+
+    def grad_pre():
+        @pl.loop(0, HB)
+        def _(k):
+            gp[k] = (segment(3, k) * slope[k]).astype(BF)
+
     own(0)
     z_send(0, 1).start()
     own(1)
-
     pull(1)
     pull(2)
     near(0)
@@ -432,98 +495,53 @@
     z_send(1, 0).start()
     partner(0, 0)
     pull(4)
+    z_send(1, 1).start()
     partner(0, 1)
     near(1)
-    z_send(1, 1).start()
     pull(5)
     far(0, 0)
     pull(6)
     far(0, 1)
+    partner(1, 0)
     pull(7)
-
-    def code_send(i):
-        to = dev((x + i) % 4, y, zl, zh, c)
-        return remote(C.at[x], C.at[x], cx_send.at[i], cx_recv.at[x], to)
-
-    for i in range(1, 4):
-        code_send(i).start()
-    partner(1, 0)
-    for i in range(1, 4):
-        xs_ = (x + i) % 4
-        to = dev(xs_, y, zl, zh, c)
-        remote(C.at[xs_], C.at[xs_], cx_send.at[i], cx_recv.at[xs_], to).wait_recv()
-    to_smem = pltpu.make_async_copy(C, codes, in_sem.at[0])
-    to_smem.start()
-    table[...] = jnp.zeros_like(table)
-    order_v[...] = jnp.zeros_like(order_v)
-    run[0] = jnp.zeros((BLK, TOK), F32)
-    for r in range(ROWS):
-        table[r : r + 1] = C[r % 4, r // 4]
-    sort_slots(UH, 0)
-    sort_slots(DH, 3)
-    order_copy = pltpu.make_async_copy(order_v, order, in_sem.at[1])
-    order_copy.start()
-    for i in range(1, 4):
-        xs_ = (x + i) % 4
-        to = dev(xs_, y, zl, zh, c)
-
-        @pl.loop(0, NZ)
-        def _(j):
-            for p in range(2):
-                ref = W.at[xs_, j, p]
-                remote(ref, ref, wx_send.at[j, i, p], wx_recv.at[xs_, j, p], to).wait_recv()
-
-    def core_wait(a):
-        @pl.loop(0, 8)
-        def _(v):
-            for h in range(2):
-                t_wait(a, 2 * v + 1 - c, h)
-
+    code_sends()
+    partner(1, 1)
+    settle()
     core_wait(0)
-    to_smem.wait()
-    order_copy.wait()
+    expand_all()
     tiles(forward)
-    partner(1, 1)
     far(1, 0)
+    far(1, 1)
     segment_sums(p1, 0)
-
-    @pl.loop(0, HB)
-    def _(k):
-        v, d = gelu_parts(segment(0, k))
-        act[k] = v.astype(BF)
-        slope[k] = d
-
-    far(1, 1)
+    gelu()
     units(mixed_tile, 0, False)
     units(mixed_tile, 0, True)
     core_wait(1)
+    wave(down_tile, 1)
+    core_stage(0)
     tiles(backward)
-    core_stage(0)
+    step(0, 1)
     segment_sums(p2, 3)
-
-    @pl.loop(0, HB)
-    def _(k):
-        gp[k] = (segment(3, k) * slope[k]).astype(BF)
-
+    grad_pre()
+    step(1, 1)
     wave(up_tile, 0)
+    step(0, 0)
     y_stage(0)
-    step(0, 0)
-    wave(down_tile, 1)
+    step(2, 1)
+    units(input_tile, 1, False)
     step(1, 0)
-    units(input_tile, 1, False)
+    step(3, 1)
+    units(input_tile, 1, True)
     step(2, 0)
-    units(input_tile, 1, True)
+    step(4, 1)
+    core_stage(1)
     step(3, 0)
-    step(0, 1)
-    core_stage(1)
+    step(5, 1)
     step(4, 0)
-    step(1, 1)
+    step(6, 1)
+    y_stage(1)
     step(5, 0)
-    step(2, 1)
-    y_stage(1)
     step(6, 0)
-    for t in range(3, 7):
-        step(t, 1)
     owns = []
     for p in range(2):
         total[...] = x_sum(zl, p)
@@ -617,7 +635,7 @@
         S((NX, NZ, 1, 128), I32), V((128, 128), I32), V((8, 128), I32), S((8, 128), I32),
         V((ROWS * CAP, BLK, TOK), F32), V((ROWS * CAP, BLK, TOK), F32), V((ROWS * CAP + 1, BLK, TOK), F32),
         V((HB, BLK, TOK), BF), V((HB, BLK, TOK), F32), V((HB, BLK, TOK), BF),
-        V((2, UNITS) + UNIT, BF), V((NX, NZ) + WTILE, BF),
+        V((2, ROWS, HALF, CAP * BLK), BF), V((2, UNITS) + UNIT, BF), V((NX, NZ) + WTILE, BF),
         V((2, 8) + UNIT, BF), V((2, 8) + UNIT, BF), V((2, 3, 2) + UNIT, BF), V((2,) + UNIT, BF), V((2,) + UNIT, BF),
         V((3, NZ) + WTILE, BF), V((NZ,) + WTILE, BF), V((NZ,) + WTILE, BF), V((NZ,) + WTILE, BF),
         V((BLK, CAP * BLK), F32),

time: 129 us -> 123 us (0.953)
  the two profiles are of different devices: /device:TPU:8 before, /device:TPU:6 now
where the time goes in v4:
time: 123 us; the launch traced here: 121 us
  Pallas kernels  116 us (94%)
  local copies, waits for them, and re-layouts  3.72 us (3%)
  between operations  1.95 us (2%)
    pallas_call x1, Pallas kernels, shards(): pl.pallas_call(kernel, name='ffn', out_shape=(jax.ShapeDtypeStruct((TOK,...  116 us
    unnamed x10, local copies, waits for them, and re-layouts  3.72 us

profile of v4, /device:TPU:6, one launch (start us, length us, event | category | flops | bytes accessed | tf_op | source)
XLA Modules:
  0.0 121.3 jit_solution(11510784864649098417)
XLA Ops:
  1.9 115.6 %ffn.1 = (bf16[128,384]{1,0:T(8,128)(2,1)}, bf16[128,384]{1,0:T(8,128)(2,1)}, bf16[64,256]{1,0:T(8,128)(2,1)}, bf16[64,256]{1,0:T(8,128)(2,1)}) custom-call(bf16[128,384]{1,0:T(8,128)(2,1)} %tok_h.1, bf16[128,384]{1,0:T(8,128)(2,1)} %grad_h.1, bf16[64,256]{1,0:T(8,128)(2,1)} %wup_h.1, bf16[64,256]{1,0:T(8,128)(2,1)} %wdn_h.1, s32[1,4]{1,0:T(1,128)} %uf_h.1, ...), custom_call_target="tpu_custom_call" | custom-call | tf_op jit(solution)/shard_map/ffn/pallas_call | solution.py:645
  117.6 0.0 copy-start
  117.6 1.6 %copy.20 = bf16[128,384]{1,0:T(8,128)(2,1)} copy(bf16[128,384]{1,0:T(8,128)(2,1)} %get-tuple-element.8) | data formatting | bytes 196608
  119.1 0.0 copy-done
  119.1 0.0 copy-start.2
  119.2 0.6 copy.21
  119.8 0.1 copy-done.2
  119.9 0.0 copy-start.1
  119.9 0.6 copy.22
  120.5 0.2 copy-done.1
  120.7 0.6 copy.23
Async XLA Ops:
  117.6 1.6 %copy-start = (bf16[128,384]{1,0:T(8,128)(2,1)S(1)}, bf16[128,384]{1,0:T(8,128)(2,1)}, u32[]{:S(2)}) copy-start(bf16[128,384]{1,0:T(8,128)(2,1)} %get-tuple-element.9) | copy-start | bytes 294916
  119.1 0.8 copy-start.2
  119.9 0.8 copy-start.1

commit v5 on v4

--- a/solution.py
+++ b/solution.py
@@ -82,7 +82,7 @@
     T0, T1, W, C, tok, grad, wup, wdn, uf, uh, uc, df, dh, dc, in_sem,
     t_send, t_recv, wz_send, wz_recv, wx_send, wx_recv, cz_send, cz_recv, cx_send, cx_recv,
     codes, table, order_v, order, p1, p2, run, act, slope, gp,
-    lhs, M, G, rc, s1, ry, s2, rz, rx, sz, rl, rr, total,
+    M, G, rc, s1, ry, s2, rz, rx, sz, rl, rr, total,
     c_send, c_recv, y_sem_send, y_sem_recv, z_sem_send, z_sem_recv, x_send, x_recv,
     l_send, l_recv, r_send, r_recv,
 ):
@@ -323,25 +323,18 @@
             which = jnp.where(lane == s, code(r, base + s), which)
         return [jnp.where(which == f, 1.0, 0.0).astype(BF) for f in range(3)]
 
-    def expand(r):
-        w = W[r % 4, r // 4, 0]
-        lhs[1, r] = jnp.concatenate([w * m for m in slot_masks(r, UF)], axis=0)
+    def mixed_tile(r):
         w = W[r % 4, r // 4, 1].astype(F32)
         w = jnp.concatenate([w[:, s * BLK : (s + 1) * BLK].T for s in range(CAP)], axis=1).astype(BF)
-        lhs[0, r] = jnp.concatenate([w * m for m in slot_masks(r, DF)], axis=0)
-
-    def mixed_tile(r):
+        lhs = jnp.concatenate([w * m for m in slot_masks(r, DF)], axis=0)
         rhs = jnp.concatenate([act[code(r, DH + s)] for s in range(CAP)], axis=0)
-        M[0, r // 2, r % 2] = dot(lhs[0, r], rhs).astype(BF)
+        M[0, r // 2, r % 2] = dot(lhs, rhs).astype(BF)
 
     def input_tile(r):
+        w = W[r % 4, r // 4, 0]
+        lhs = jnp.concatenate([w * m for m in slot_masks(r, UF)], axis=0)
         rhs = jnp.concatenate([gp[code(r, UH + s)] for s in range(CAP)], axis=0)
-        M[1, r // 2, r % 2] = dot(lhs[1, r], rhs).astype(BF)
-
-    def expand_all():
-        @pl.loop(0, ROWS, unroll=2)
-        def _(r):
-            expand(r)
+        M[1, r // 2, r % 2] = dot(lhs, rhs).astype(BF)
 
     def down_tile(j, xx):
         r = j * 4 + xx
@@ -508,16 +501,15 @@
     partner(1, 1)
     settle()
     core_wait(0)
-    expand_all()
     tiles(forward)
     far(1, 0)
     far(1, 1)
     segment_sums(p1, 0)
     gelu()
     units(mixed_tile, 0, False)
-    units(mixed_tile, 0, True)
     core_wait(1)
     wave(down_tile, 1)
+    units(mixed_tile, 0, True)
     core_stage(0)
     tiles(backward)
     step(0, 1)
@@ -635,7 +627,7 @@
         S((NX, NZ, 1, 128), I32), V((128, 128), I32), V((8, 128), I32), S((8, 128), I32),
         V((ROWS * CAP, BLK, TOK), F32), V((ROWS * CAP, BLK, TOK), F32), V((ROWS * CAP + 1, BLK, TOK), F32),
         V((HB, BLK, TOK), BF), V((HB, BLK, TOK), F32), V((HB, BLK, TOK), BF),
-        V((2, ROWS, HALF, CAP * BLK), BF), V((2, UNITS) + UNIT, BF), V((NX, NZ) + WTILE, BF),
+        V((2, UNITS) + UNIT, BF), V((NX, NZ) + WTILE, BF),
         V((2, 8) + UNIT, BF), V((2, 8) + UNIT, BF), V((2, 3, 2) + UNIT, BF), V((2,) + UNIT, BF), V((2,) + UNIT, BF),
         V((3, NZ) + WTILE, BF), V((NZ,) + WTILE, BF), V((NZ,) + WTILE, BF), V((NZ,) + WTILE, BF),
         V((BLK, CAP * BLK), F32),

time: 123 us -> 120 us (0.976)
  Pallas kernels: 116 us -> 113 us
    pallas_call x1, Pallas kernels: 116 us -> 113 us  [shards(): pl.pallas_call(kernel, name='ffn', out_shape=(jax.ShapeDtypeStruct((TOK,...]
where the time goes in v5:
time: 120 us; the launch traced here: 118 us
  Pallas kernels  113 us (94%)
  local copies, waits for them, and re-layouts  3.72 us (3%)
  between operations  1.95 us (2%)
    pallas_call x1, Pallas kernels, shards(): pl.pallas_call(kernel, name='ffn', out_shape=(jax.ShapeDtypeStruct((TOK,...  113 us
    unnamed x10, local copies, waits for them, and re-layouts  3.72 us

profile of v5, /device:TPU:6, one launch (start us, length us, event | category | flops | bytes accessed | tf_op | source)
XLA Modules:
  0.0 118.5 jit_solution(14982453044856978262)
XLA Ops:
  1.9 112.8 %ffn.1 = (bf16[128,384]{1,0:T(8,128)(2,1)}, bf16[128,384]{1,0:T(8,128)(2,1)}, bf16[64,256]{1,0:T(8,128)(2,1)}, bf16[64,256]{1,0:T(8,128)(2,1)}) custom-call(bf16[128,384]{1,0:T(8,128)(2,1)} %tok_h.1, bf16[128,384]{1,0:T(8,128)(2,1)} %grad_h.1, bf16[64,256]{1,0:T(8,128)(2,1)} %wup_h.1, bf16[64,256]{1,0:T(8,128)(2,1)} %wdn_h.1, s32[1,4]{1,0:T(1,128)} %uf_h.1, ...), custom_call_target="tpu_custom_call" | custom-call | tf_op jit(solution)/shard_map/ffn/pallas_call | solution.py:637
  114.7 0.0 copy-start
  114.8 1.6 %copy.20 = bf16[128,384]{1,0:T(8,128)(2,1)} copy(bf16[128,384]{1,0:T(8,128)(2,1)} %get-tuple-element.8) | data formatting | bytes 196608
  116.3 0.0 copy-done
  116.3 0.0 copy-start.2
  116.3 0.6 copy.21
  117.0 0.1 copy-done.2
  117.1 0.0 copy-start.1
  117.1 0.6 copy.22
  117.7 0.2 copy-done.1
  117.9 0.6 copy.23
Async XLA Ops:
  114.7 1.6 %copy-start = (bf16[128,384]{1,0:T(8,128)(2,1)S(1)}, bf16[128,384]{1,0:T(8,128)(2,1)}, u32[]{:S(2)}) copy-start(bf16[128,384]{1,0:T(8,128)(2,1)} %get-tuple-element.9) | copy-start | bytes 294916
  116.3 0.8 copy-start.2
  117.1 0.8 copy-start.1
